TPU v7x, 32 devices: a whole 2x2x4 slice. The times are simulated.
32 devices in a mesh: dp: 16 (over z, y, x), mp: 2 (over core).
Axes of the slice: x: 2, y: 2, z: 4, core: 2. Of those that a mesh axis runs over, the one named last changes fastest.
Arguments:
- query_emb: bfloat16 [128, 4096], P('dp', 'mp'), as said below
- item_emb: bfloat16 [128, 4096], P('dp', 'mp'), as said below
- pair_index: int32 [128], P('dp'), may hold values from 0 to 127, each once
- hard_index: int32 [128, 4], P('dp'), may hold values from 0 to 127
- hidden_in: bfloat16 [2, 16, 152, 4096], P(None, 'dp', None, 'mp'), may hold values from -24 to 24
- lengths: int32 [2, 16], P(None, 'dp'), may hold values from 76 to 152
- w_query: bfloat16 [4096, 4096], P('dp', 'mp'), as said below
- key_weight_matrix: bfloat16 [4096, 1024], P(None, 'mp'), as said below
- value_weight_matrix: bfloat16 [4096, 1024], P(None, 'mp'), may hold values from -0.09375 to 0.09375
- w_out: bfloat16 [4096, 4096], P('mp', 'dp'), may hold values from -0.09375 to 0.09375
- key_down_matrix: bfloat16 [4096, 16], replicated, may hold values from -0.09375 to 0.09375
- key_up_matrix: bfloat16 [16, 1024], P(None, 'mp'), may hold values from -0.29882812 to 0.29882812
- value_down: bfloat16 [4096, 16], replicated, may hold values from -0.09375 to 0.09375
- value_up_matrix: bfloat16 [16, 1024], P(None, 'mp'), may hold values from -0.29882812 to 0.29882812
Outputs:
- mean_loss: float32 [], replicated
- query_grad: bfloat16 [128, 4096], P('dp', 'mp')
- item_grad: bfloat16 [128, 4096], P('dp', 'mp')
- input_grad: bfloat16 [2, 16, 152, 4096], P(None, 'dp', None, 'mp')
- key_down_grad: float32 [4096, 16], replicated
- value_down_grad: float32 [4096, 16], replicated
- key_up_grad: float32 [16, 1024], P(None, 'mp')
- value_up_grad: float32 [16, 1024], P(None, 'mp')
Inputs may be any that keep to these rules, and one draw needn't show every extreme that they name: `query_emb`: entries within 10 / sqrt(4096) in magnitude. `item_emb`: entries within 10 / sqrt(4096) in magnitude. `w_query`: entries within 16 / sqrt(4096) in magnitude. `key_weight_matrix`: entries within 6 / sqrt(4096) in magnitude.
All inputs are finite; a program needn't handle non-finite values.
Results may differ from a plain program's by a relative error of at most 0.025.
The roundings to bfloat16 on the way count: a program that leaves them out, or rounds other values in their place, can miss the bound.
Values may be sent and summed in bfloat16 or wider, within the bound.
A program may use at most 128 MiB of HBM per device.

v0:
```python
import math

import jax
import jax.numpy as jnp
from jax import lax
from jax.sharding import PartitionSpec as P

HEADS = 32
KV_HEADS = 8
HEAD_DIM = 128


INV_TEMP = 50.0
HARD_NEGATIVE_ADD = 4.0
ADAPTER_SCALE = 2.0


def final_product(left_side, right_side):
    return lax.dot_general(
        left_side, right_side, (((1,), (1,)), ((), ())), preferred_element_type=jnp.float32
    )


def first_product(left_side, right_side):
    return lax.dot_general(
        left_side, right_side, (((0,), (0,)), ((), ())), preferred_element_type=jnp.float32
    )


def local(
    query_emb,
    item_emb,
    pair_index,
    hard_index,
    hidden_in,
    lengths,
    w_query,
    key_weight_matrix,
    value_weight_matrix,
    w_out,
    key_down_matrix,
    key_up_matrix,
    value_down,
    value_up_matrix,
):
    dp_count = lax.axis_size("dp")
    local_rows = query_emb.shape[0]
    batch_size = local_rows * dp_count
    items_all = lax.all_gather(item_emb, "dp", axis=0, tiled=True)
    partial_scores = final_product(query_emb, items_all)
    pair_scores = lax.psum(partial_scores, "mp") * INV_TEMP
    columns = jnp.arange(batch_size, dtype=jnp.int32)
    hard_negative_count = jnp.sum(
        (hard_index[:, :, None] == columns[None, None, :]).astype(jnp.float32), axis=1
    )
    score_logits = pair_scores + HARD_NEGATIVE_ADD * hard_negative_count
    row_top = jnp.max(score_logits, axis=1, keepdims=True)
    log_total = row_top[:, 0] + jnp.log(jnp.sum(jnp.exp(score_logits - row_top), axis=1))
    target = (pair_index[:, None] == columns[None, :]).astype(jnp.float32)
    picked = jnp.sum(target * score_logits, axis=1)
    loss_part = jnp.sum(log_total - picked)
    residual = (jnp.exp(score_logits - log_total[:, None]) - target).astype(jnp.bfloat16)
    query_grad = (
        jnp.dot(residual, items_all, preferred_element_type=jnp.float32) * INV_TEMP
    ).astype(jnp.bfloat16)
    item_grad = lax.psum_scatter(
        first_product(residual, query_emb) * INV_TEMP, "dp", scatter_dimension=0, tiled=True
    ).astype(jnp.bfloat16)
    sub_count = hidden_in.shape[0]
    seq_len = hidden_in.shape[2]
    full_rows = lax.all_gather(hidden_in, "mp", axis=3, tiled=True)
    model_width = full_rows.shape[3]
    token_inputs = full_rows.reshape(sub_count * seq_len, model_width)
    seq_lengths = lengths[:, 0]
    last_rows = jnp.arange(sub_count, dtype=jnp.int32) * seq_len + seq_lengths - 1
    last_tokens = jnp.take(token_inputs, last_rows, axis=0)
    cot_local = item_grad[:sub_count]
    cot_full = lax.all_gather(cot_local, "mp", axis=1, tiled=True)
    adapter_rank = key_down_matrix.shape[1]
    down_both = jnp.concatenate([key_down_matrix, value_down], axis=1)
    reduced_pair = jnp.dot(token_inputs, down_both, preferred_element_type=jnp.float32).astype(
        jnp.bfloat16
    )
    reduced_key = reduced_pair[:, :adapter_rank]
    reduced_value = reduced_pair[:, adapter_rank:]
    key_rows = (
        jnp.dot(token_inputs, key_weight_matrix, preferred_element_type=jnp.float32)
        + ADAPTER_SCALE * jnp.dot(reduced_key, key_up_matrix, preferred_element_type=jnp.float32)
    ).astype(jnp.bfloat16)
    value_rows = (
        jnp.dot(token_inputs, value_weight_matrix, preferred_element_type=jnp.float32)
        + ADAPTER_SCALE
        * jnp.dot(reduced_value, value_up_matrix, preferred_element_type=jnp.float32)
    ).astype(jnp.bfloat16)
    query_width = w_query.shape[1]
    wq_full, wo_full = (
        lax.all_gather(w_query, "dp", axis=0, tiled=True),
        lax.all_gather(w_out, "dp", axis=1, tiled=True),
    )
    query = jnp.dot(last_tokens, wq_full, preferred_element_type=jnp.float32).astype(jnp.bfloat16)
    attn_grad = final_product(cot_full, wo_full).astype(jnp.bfloat16)
    group_size = HEADS // KV_HEADS
    kv_local = key_rows.shape[1] // HEAD_DIM
    score_scale = 1.0 / math.sqrt(HEAD_DIM)
    q_heads = query.reshape(sub_count, kv_local, group_size, HEAD_DIM)
    k_heads = key_rows.reshape(sub_count, seq_len, kv_local, HEAD_DIM)
    v_heads = value_rows.reshape(sub_count, seq_len, kv_local, HEAD_DIM)
    raw_scores = (
        jnp.einsum("bkgd,bjkd->bkgj", q_heads, k_heads, preferred_element_type=jnp.float32)
        * score_scale
    )
    live_mask = jnp.arange(seq_len, dtype=jnp.int32)[None, :] < seq_lengths[:, None]
    raw_scores = jnp.where(live_mask[:, None, None, :], raw_scores, -jnp.inf)
    row_peak = jnp.max(raw_scores, axis=-1, keepdims=True)
    weights = jnp.exp(raw_scores - row_peak)
    softmax_probs = weights / jnp.sum(weights, axis=-1, keepdims=True)
    prob_half = softmax_probs.astype(jnp.bfloat16)
    grad_heads = attn_grad.reshape(sub_count, kv_local, group_size, HEAD_DIM)
    prob_grad = jnp.einsum(
        "bkgd,bjkd->bkgj", grad_heads, v_heads, preferred_element_type=jnp.float32
    )
    score_grad = (
        softmax_probs
        * (prob_grad - jnp.sum(softmax_probs * prob_grad, axis=-1, keepdims=True))
        * score_scale
    ).astype(jnp.bfloat16)
    query_delta = (
        jnp.einsum("bkgj,bjkd->bkgd", score_grad, k_heads, preferred_element_type=jnp.float32)
        .astype(jnp.bfloat16)
        .reshape(sub_count, query_width)
    )
    key_adapter_change = (
        jnp.einsum("bkgj,bkgd->bjkd", score_grad, q_heads, preferred_element_type=jnp.float32)
        .astype(jnp.bfloat16)
        .reshape(sub_count * seq_len, kv_local * HEAD_DIM)
    )
    value_adapter_change = (
        jnp.einsum("bkgj,bkgd->bjkd", prob_half, grad_heads, preferred_element_type=jnp.float32)
        .astype(jnp.bfloat16)
        .reshape(sub_count * seq_len, kv_local * HEAD_DIM)
    )
    last_part = final_product(query_delta, wq_full)
    key_coefficient = final_product(key_adapter_change, key_up_matrix).astype(jnp.bfloat16)
    value_coefficient = final_product(value_adapter_change, value_up_matrix).astype(jnp.bfloat16)
    input_portion = final_product(key_adapter_change, key_weight_matrix) + final_product(
        value_adapter_change, value_weight_matrix
    )
    input_portion = input_portion + ADAPTER_SCALE * (
        final_product(key_coefficient, key_down_matrix)
        + final_product(value_coefficient, value_down)
    )
    input_portion = input_portion.at[last_rows].add(last_part)
    input_sum = lax.psum_scatter(
        input_portion.astype(jnp.bfloat16), "mp", scatter_dimension=1, tiled=True
    ).astype(jnp.float32)
    input_sum = input_sum.at[last_rows].add(cot_local.astype(jnp.float32))
    input_grad = input_sum.astype(jnp.bfloat16).reshape(hidden_in.shape)
    key_down_grad, value_down_grad = lax.psum(
        (
            ADAPTER_SCALE * first_product(token_inputs, key_coefficient),
            ADAPTER_SCALE * first_product(token_inputs, value_coefficient),
        ),
        ("dp", "mp"),
    )
    total_loss, key_up_grad, value_up_grad = lax.psum(
        (
            loss_part,
            ADAPTER_SCALE * first_product(reduced_key, key_adapter_change),
            ADAPTER_SCALE * first_product(reduced_value, value_adapter_change),
        ),
        "dp",
    )
    mean_loss = total_loss / batch_size
    return (
        mean_loss,
        query_grad,
        item_grad,
        input_grad,
        key_down_grad,
        value_down_grad,
        key_up_grad,
        value_up_grad,
    )


def solution(mesh):
    in_specs = (
        P("dp", "mp"),
        P("dp", "mp"),
        P("dp"),
        P("dp", None),
        P(None, "dp", None, "mp"),
        P(None, "dp"),
        P("dp", "mp"),
        P(None, "mp"),
        P(None, "mp"),
        P("mp", "dp"),
        P(),
        P(None, "mp"),
        P(),
        P(None, "mp"),
    )
    out_specs = (
        P(),
        P("dp", "mp"),
        P("dp", "mp"),
        P(None, "dp", None, "mp"),
        P(),
        P(),
        P(None, "mp"),
        P(None, "mp"),
    )
    return jax.shard_map(local, mesh=mesh, in_specs=in_specs, out_specs=out_specs, check_vma=False)
```

profile of v0, /device:TPU:0, one launch (start us, length us, event | category | flops | bytes accessed | tf_op | source)
XLA Modules:
  0.0 714.1 jit_solution(5097832709535216510)
XLA Ops:
  8.1 45.7 %all_gather.15 = bf16[128,2048]{1,0:T(8,128)(2,1)S(1)} all-gather(bf16[8,2048]{1,0:T(8,128)(2,1)} %param.15), channel_id=1, replica_groups=mesh['dp'=16,'mp'=2] {'dp'}, dimensions={0}, use_global_device_ids=true | all-gather | bytes 557056 | tf_op jit(solution)/shard_map/all_gather | solution.py:49
  54.0 2.4 psum.42
  56.5 0.8 convert_reduce_fusion
  57.4 0.9 select_reduce_fusion
  58.2 0.6 subtract_reduce_fusion
  58.9 2.0 convolution_multiply_fusion.2
  62.8 0.6 iota_compare_fusion.2
  63.4 161.9 %reduce-scatter.3.cloned.1.call-done = f32[8,2048]{1,0:T(8,128)} async-done(((f32[128,2048]{1,0:T(8,128)}), f32[8,2048]{1,0:T(8,128)}) %reduce-scatter.3.cloned.1.call-update) | async-done | bytes 65552 | tf_op jit(solution)/shard_map/reduce_scatter | solution.py:66
  225.3 0.8 convert_element_type.76
  226.1 1.9 all_gather.18
  228.1 2.5 fusion.20
  230.7 4.6 fusion.66
  235.3 1.0 fusion.10
  236.3 1.0 reshape.89
  237.4 3.6 fusion.65
  241.0 1.0 fusion.9
  242.0 1.8 reshape.87
  244.3 67.5 %all-gather.8.cloned.1.call-done = bf16[2048,4096]{1,0:T(8,128)(2,1)} async-done(((bf16[2048,256]{1,0:T(8,128)(2,1)}), bf16[2048,4096]{1,0:T(8,128)(2,1)}) %all-gather.8.cloned.1.call-update) | async-done | bytes 16777232 | tf_op jit(solution)/shard_map/all_gather | solution.py:98
  311.9 10.2 %convolution_convert_fusion = bf16[2,2048]{1,0:T(2,128)(2,1)S(1)} fusion(bf16[2,4096]{1,0:T(2,128)(2,1)} %all_gather.18, bf16[2048,4096]{1,0:T(8,128)(2,1)} %all-gather.8.cloned.1.call-done), kind=kOutput, calls=%fused_computation.16 | convolution fusion | flops 33558528 | bytes 16801792 | tf_op jit(solution)/shard_map/dot_general | solution.py:19
  322.1 182.1 %all-gather.6.cloned.1.call-done = bf16[4096,2048]{1,0:T(8,128)(2,1)} async-done(((bf16[256,2048]{1,0:T(8,128)(2,1)}), bf16[4096,2048]{1,0:T(8,128)(2,1)}) %all-gather.6.cloned.1.call-update) | async-done | bytes 16777232 | tf_op jit(solution)/shard_map/all_gather | solution.py:97
  504.2 8.1 %convolution_convert_fusion.1 = bf16[2,2048]{1,0:T(2,128)(2,1)S(1)} fusion(bf16[4096,2048]{1,0:T(8,128)(2,1)} %all-gather.6.cloned.1.call-done, bf16[2,4096]{1,0:T(2,128)(2,1)S(1)} %gather_fusion, pred[2]{0:T(512)(128)(4,1)S(1)} %get-tuple-element.39), kind=kOutput, calls=%fused_computation.17 | convolution fusion | flops 33566720 | bytes 16801794 | tf_op jit(solution)/shard_map/dot_general | solution.py:100
  512.2 1.2 fusion.18
  513.5 0.7 fusion.63
  514.2 0.9 fusion.28
  515.1 2.1 fusion.12
  517.2 2.1 fusion.11
  519.3 1.1 copy.36
  520.4 5.9 fusion.26
  526.5 2.0 convolution_convert_fusion.7
  528.6 1.1 copy.37
  529.7 0.9 convolution_convert_fusion.5
  530.6 7.7 %convolution_add_fusion.1 = f32[304,4096]{1,0:T(8,128)} fusion(f32[304,4096]{1,0:T(8,128)} %fusion.26, bf16[4096,512]{1,0:T(8,128)(2,1)} %param.22, bf16[38,8,4,128]{3,2,1,0:T(4,128)(2,1)S(1)} %bitcast.80), kind=kOutput, calls=%fused_computation.8 | convolution fusion | flops 1276313600 | bytes 14467072 | tf_op jit(solution)/shard_map/dot_general | solution.py:19
  538.2 3.1 fusion.67
  541.4 0.7 reshape.92
  542.1 7.0 fusion.3
  549.1 10.2 %fusion.68 = f32[2,4096]{1,0:T(2,128)S(1)} fusion(bf16[2,2048]{1,0:T(2,128)(2,1)S(1)} %reshape.92, bf16[4096,2048]{1,0:T(8,128)(2,1)} %all-gather.6.cloned.1.call-done), kind=kOutput, calls=%fused_computation.104 | convolution fusion | flops 33554432 | bytes 16818176 | tf_op jit(solution)/shard_map/dot_general | solution.py:19
  559.3 5.2 scatter_fusion
  564.5 4.2 convert_element_type.92
  568.8 0.9 fusion.6
  569.7 1.2 fusion.5
  570.9 1.2 fusion.4
  572.5 76.1 %all-reduce.6 = (f32[]{:T(128)}, f32[16,512]{1,0:T(8,128)}, f32[16,512]{1,0:T(8,128)}) all-reduce(f32[]{:T(128)} %get-tuple-element.41, f32[16,512]{1,0:T(8,128)S(1)} %convolution_multiply_fusion.7, f32[16,512]{1,0:T(8,128)S(1)} %convolution_multiply_fusion.6), channel_id=1, replica_groups=mesh['dp'=16,'mp'=2] {'dp'}, use_global_device_ids=true, to_apply=%region_6.0 | all-reduce | flops 16385 | bytes 131080 | tf_op jit(solution)/shard_map/psum | solution.py:165
  649.3 1.6 convert_element_type.93
  650.9 1.5 scatter_custom_fusion.1
  652.4 1.2 convert_element_type.95
  653.6 48.4 %all-reduce.5.cloned.1.call-done = (f32[4096,16]{0,1:T(8,128)}, f32[4096,16]{0,1:T(8,128)}) async-done(((f32[4096,16]{0,1:T(8,128)}, f32[4096,16]{0,1:T(8,128)}), (f32[4096,16]{0,1:T(8,128)}, f32[4096,16]{0,1:T(8,128)})) %all-reduce.5.cloned.1.call-update) | async-done | bytes 524304 | tf_op jit(solution)/shard_map/psum | solution.py:158
  702.0 1.7 copy.79
  703.7 1.7 copy.80
  (61 shorter events, 3.5 us)
Async XLA Ops:
  8.0 45.8 %copy-start = (bf16[8,2048]{1,0:T(8,128)(2,1)S(1)}, bf16[8,2048]{1,0:T(8,128)(2,1)}, u32[]{:S(2)}) copy-start(bf16[8,2048]{1,0:T(8,128)(2,1)} %param.14) | copy-start | bytes 98308
  8.0 54.7 %copy-start.17 = (s32[2,1]{0,1:T(1,128)S(1)}, s32[2,1]{0,1:T(1,128)}, u32[]{:S(2)}) copy-start(s32[2,1]{0,1:T(1,128)} %param.19) | copy-start | bytes 28
  8.0 220.1 %copy-start.5 = (bf16[4096,16]{0,1:T(8,128)(2,1)S(1)}, bf16[4096,16]{0,1:T(8,128)(2,1)}, u32[]{:S(2)}) copy-start(bf16[4096,16]{0,1:T(8,128)(2,1)} %param.24) | copy-start | bytes 393220
  8.0 220.1 %copy-start.6 = (bf16[4096,16]{0,1:T(8,128)(2,1)S(1)}, bf16[4096,16]{0,1:T(8,128)(2,1)}, u32[]{:S(2)}) copy-start(bf16[4096,16]{0,1:T(8,128)(2,1)} %param.26) | copy-start | bytes 393220
  8.0 217.2 %reduce-scatter.3.cloned.1.call-start = ((), (), s32[]{:S(2)}) async-start(), calls=%async_computation.2 | async-start | bytes 1114112 | tf_op jit(solution)/shard_map/reduce_scatter | solution.py:66
  58.9 166.4 %copy-start.13 = (f32[8]{0:T(128)}, f32[8]{0:T(128)S(1)}, u32[]{:S(2)}) copy-start(f32[8]{0:T(128)S(1)} %get-tuple-element.42) | copy-start | bytes 100
  60.9 167.2 %all-gather.4.cloned.1.call-start = ((), (), s32[]{:S(2)}) async-start(), calls=%async_computation.3 | async-start | bytes 3735552 | tf_op jit(solution)/shard_map/all_gather | solution.py:71
  61.5 250.3 %all-gather.8.cloned.1.call-start = ((), (), s32[]{:S(2)}) async-start(), calls=%async_computation.5 | async-start | bytes 17825792 | tf_op jit(solution)/shard_map/all_gather | solution.py:98
  62.1 442.1 %all-gather.6.cloned.1.call-start = ((), (), s32[]{:S(2)}) async-start(), calls=%async_computation.4 | async-start | bytes 17825792 | tf_op jit(solution)/shard_map/all_gather | solution.py:97
  62.7 586.6 %reduce-scatter.5.cloned.1.call-start = ((), (), s32[]{:S(2)}) async-start(), calls=%async_computation.6 | async-start | bytes 3735552 | tf_op jit(solution)/shard_map/reduce_scatter | solution.py:153
  62.8 172.5 %copy-start.15 = (s32[2,1]{0,1:T(1,128)}, s32[2,1]{0,1:T(1,128)S(1)}, u32[]{:S(2)}) copy-start(s32[2,1]{0,1:T(1,128)S(1)} %get-tuple-element.40) | copy-start | bytes 28
  226.1 424.7 %copy-start.7 = (bf16[8,2048]{1,0:T(8,128)(2,1)}, bf16[8,2048]{1,0:T(8,128)(2,1)S(1)}, u32[]{:S(2)}) copy-start(bf16[8,2048]{1,0:T(8,128)(2,1)S(1)} %convert_element_type.76) | copy-start | bytes 98308
  230.7 4.6 copy-start.11
  230.7 6.6 copy-start.2
  237.4 3.7 copy-start.9
  513.5 1.6 copy-start.8
  520.4 5.9 copy-start.10
  529.7 8.6 %copy-start.3 = (bf16[2,152,4,128]{3,2,1,0:T(4,128)(2,1)}, bf16[2,152,4,128]{3,2,1,0:T(4,128)(2,1)S(1)}, u32[]{:S(2)}) copy-start(bf16[2,152,4,128]{3,2,1,0:T(4,128)(2,1)S(1)} %copy.37) | copy-start | bytes 933892
  549.1 10.2 %copy-start.16 = (s32[2,1]{0,1:T(1,128)S(1)}, s32[2,1]{0,1:T(1,128)}, u32[]{:S(2)}) copy-start(s32[2,1]{0,1:T(1,128)} %copy-done.15) | copy-start | bytes 28
  564.5 4.3 copy-start.12
  564.5 4.3 copy-start.14
  568.8 133.2 %all-reduce.5.cloned.1.call-start = ((), (), s32[]{:S(2)}) async-start(), calls=%async_computation.7 | async-start | bytes 1048576 | tf_op jit(solution)/shard_map/psum | solution.py:158
  569.7 2.6 copy-start.4
  649.2 56.1 %copy-start.1 = (bf16[8,2048]{1,0:T(8,128)(2,1)S(1)}, bf16[8,2048]{1,0:T(8,128)(2,1)}, u32[]{:S(2)}) copy-start(bf16[8,2048]{1,0:T(8,128)(2,1)} %param.14) | copy-start | bytes 98308
Sparse Core Ops, SparseCore 0:
  61.0 164.1 reduce-scatter.2
  575.6 126.3 all-reduce.4
Sparse Core Ops, SparseCore 1:
  62.9 6.9 all-gather.3
  72.5 239.3 all-gather.7
  314.5 189.6 all-gather.5
  568.8 8.1 reduce-scatter.4
where the time goes:
time: 715 us; the launch traced here: 714 us
  waiting for transfers between devices  461 us (64%)
  blocking collectives  126 us (18%)
  matrix products  80.3 us (11%)
  other arithmetic  18.4 us (3%)
  between operations  17.8 us (2%)
  local copies, waits for them, and re-layouts  9.75 us (1%)
    all_gather x1, waiting for transfers between devices, local(): lax.all_gather(w_query, 'dp', axis=0, tiled=True)  182 us
    reduce_scatter x1, waiting for transfers between devices, local(): lax.psum_scatter(first_product(residual, query_emb) * INV_TEMP, 'dp', sca...  162 us
    psum x1, blocking collectives, local(): lax.psum((loss_part, ADAPTER_SCALE * first_product(reduced_key, key_adapt...  76.1 us
    all_gather x1, waiting for transfers between devices, local(): lax.all_gather(w_out, 'dp', axis=1, tiled=True)  67.5 us
    psum x1, waiting for transfers between devices, local(): lax.psum((ADAPTER_SCALE * first_product(token_inputs, key_coefficient), A...  48.4 us
    all_gather x1, blocking collectives, local(): items_all = lax.all_gather(item_emb, 'dp', axis=0, tiled=True)  45.7 us
    dot_general x9, matrix products, final_product(): lax.dot_general(left_side, right_side, (((1,), (1,)), ((), ())), preferre...  45.5 us
  transfers between devices with their start and end apart: 6, of which 4 were waited for; matrix products, arithmetic and copies ran while one was open for 5% of the time, Pallas kernels for 0%

commit v1 on v0

--- a/solution.py
+++ b/solution.py
@@ -1,8 +1,11 @@
+import functools
 import math
 
 import jax
 import jax.numpy as jnp
 from jax import lax
+from jax.experimental import pallas as pl
+from jax.experimental.pallas import tpu as pltpu
 from jax.sharding import PartitionSpec as P
 
 HEADS = 32
@@ -183,6 +186,476 @@
     )
 
 
+TILE = 512
+EMB, IDX, XS, QP, CS, AP, QD, LP, DN, UP, DNG, UPG = range(12)
+M_XL, M_X, M_SC, M_COT, M_COEF, M_PART, M_LAST, M_DN = range(8)
+
+
+def plain_product(left_side, right_side):
+    return jnp.dot(left_side, right_side, preferred_element_type=jnp.float32)
+
+
+def step_kernel(
+    dp, mp, subs, rank,
+    len_ref, emb_ref, idx_ref, x_hbm, wq_hbm, wk_hbm, wv_hbm, wo_hbm, down_ref, kup_ref, vup_ref,
+    loss_ref, emb_grad_ref, input_grad_ref, down_out, up_out,
+    emb_all, idx_all, xg, xl_g, xs, xr, x_rows, part_q, land_q, cot_g, cs, cr, cot_rows,
+    part_a, land_a, scores_g, sym, wq, wk, wv, wo, acc_k, acc_v, acc_low, q_blk, g_blk,
+    query_f, grad_f, qd_own, qd_all, qd_rows, lp, lp_land, coef_g, pacc, pbuf, pland, last_rows_f,
+    last_send, last_land, dn, dn_land, up, up_land, last_total, ssem, rsem, msend, mrecv, csem,
+):
+    me = lax.axis_index("dp")
+    core = lax.axis_index("mp")
+    other = 1 - core
+    rows, feats = x_hbm.shape
+    seq_len = rows // subs
+    group_rows = emb_ref.shape[0]
+    half_rows = group_rows // 2
+    total_rows = dp * group_rows
+    dq, qw = wq.shape
+    kw = wk.shape[1]
+    tiles = feats // TILE
+
+    local_copies = [
+        pltpu.make_async_copy(src, dst, csem.at[i])
+        for i, (src, dst) in enumerate(
+            ((x_hbm, xg.at[core]), (wq_hbm, wq), (wk_hbm, wk), (wv_hbm, wv), (wo_hbm, wo))
+        )
+    ]
+    for copy in local_copies:
+        copy.start()
+
+    barrier = pltpu.get_barrier_semaphore()
+
+    @pl.loop(1, dp)
+    def _(k):
+        pl.semaphore_signal(
+            barrier, inc=1, device_id=(lax.rem(me + k, dp), core), device_id_type=pl.DeviceIdType.MESH
+        )
+
+    pl.semaphore_signal(barrier, inc=1, device_id=(me, other), device_id_type=pl.DeviceIdType.MESH)
+    pl.semaphore_wait(barrier, dp)
+
+    def dp_copy(op, k, source, landing):
+        target = lax.rem(me + k, dp)
+        return pltpu.make_async_remote_copy(
+            src_ref=source(target),
+            dst_ref=landing.at[me],
+            send_sem=ssem.at[op, k],
+            recv_sem=rsem.at[op, k],
+            device_id=(target, core),
+            device_id_type=pl.DeviceIdType.MESH,
+        )
+
+    def dp_start(op, source, landing):
+        @pl.loop(1, dp)
+        def _(k):
+            dp_copy(op, k, source, landing).start()
+
+    def dp_wait(op, source, landing):
+        @pl.loop(1, dp)
+        def _(k):
+            dp_copy(op, k, source, landing).wait()
+
+    def mp_copy(op, source, landing):
+        return pltpu.make_async_remote_copy(
+            src_ref=source,
+            dst_ref=landing,
+            send_sem=msend.at[op],
+            recv_sem=mrecv.at[op],
+            device_id=(me, other),
+            device_id_type=pl.DeviceIdType.MESH,
+        )
+
+    emb_args = (EMB, lambda t: emb_ref, emb_all)
+    idx_args = (IDX, lambda t: idx_ref, idx_all)
+    dp_start(*emb_args)
+    dp_start(*idx_args)
+    emb_all[me] = emb_ref[...]
+    idx_all[me] = idx_ref[...]
+
+    local_copies[0].wait()
+    last = [jnp.clip(len_ref[b] - 1, 0, seq_len - 1) + b * seq_len for b in range(subs)]
+    one_row = lax.broadcasted_iota(jnp.int32, (8, rows), 0)
+    one_col = lax.broadcasted_iota(jnp.int32, (8, rows), 1)
+    picked_rows = jnp.zeros((8, rows), jnp.float32)
+    for b in range(subs):
+        picked_rows = jnp.where((one_row == b) & (one_col == last[b]), 1.0, picked_rows)
+    xl_g[core] = plain_product(picked_rows.astype(jnp.bfloat16), xg[core])[:subs]
+    xl_copy = mp_copy(M_XL, xl_g.at[core], xl_g.at[core])
+    xl_copy.start()
+    x_copy = mp_copy(M_X, xg.at[core], xg.at[core])
+    x_copy.start()
+    xl_copy.wait()
+    per_core = dp // mp
+    for j in range(dp):
+        start = (j % per_core) * dq
+        xs[j] = xl_g[j // per_core, :, start : start + dq]
+    xs_args = (XS, lambda t: xs.at[t], xr)
+    dp_start(*xs_args)
+    xr[me] = xs[me]
+
+    dp_wait(*emb_args)
+    dp_wait(*idx_args)
+    emb_rows = emb_all[...].reshape(total_rows, feats)
+    scores_g[core] = final_product(emb_rows, emb_rows)
+    score_copy = mp_copy(M_SC, scores_g.at[core], scores_g.at[core])
+    score_copy.start()
+
+    dp_wait(*xs_args)
+    for j in range(dp):
+        x_rows[j * subs : (j + 1) * subs, :] = xr[j]
+    local_copies[1].wait()
+    query_part = plain_product(x_rows[...].astype(jnp.bfloat16), wq[...])
+    for j in range(dp):
+        part_q[j] = query_part[j * subs : (j + 1) * subs]
+    q_args = (QP, lambda t: part_q.at[t], land_q)
+    dp_start(*q_args)
+    land_q[me] = part_q[me]
+
+    score_copy.wait()
+    logits = (scores_g[0] + scores_g[1]) * INV_TEMP
+    columns = lax.broadcasted_iota(jnp.int32, (total_rows, total_rows), 1)
+    row_ids = lax.broadcasted_iota(jnp.int32, (total_rows, total_rows), 0)
+    index_rows = idx_all[...].reshape(total_rows, idx_ref.shape[1])
+    hard_count = jnp.zeros((total_rows, total_rows), jnp.float32)
+    for h in range(4):
+        hard_count = hard_count + jnp.where(columns == index_rows[:, h + 1 : h + 2], 1.0, 0.0)
+    logits = logits + HARD_NEGATIVE_ADD * hard_count
+    is_item = lax.rem(columns, group_rows) >= half_rows
+    is_query = lax.rem(row_ids, group_rows) < half_rows
+    live_logits = jnp.where(is_item, logits, -jnp.inf)
+    row_top = jnp.max(live_logits, axis=1, keepdims=True)
+    log_total = row_top + jnp.log(jnp.sum(jnp.exp(live_logits - row_top), axis=1, keepdims=True))
+    target = jnp.where(columns == index_rows[:, 0:1], 1.0, 0.0)
+    picked = jnp.sum(target * logits, axis=1, keepdims=True)
+    loss_rows = jnp.where(is_query[:, 0:1], log_total - picked, 0.0)
+    loss_total = jnp.sum(loss_rows, axis=0, keepdims=True) / (total_rows // 2)
+    loss_ref[...] = jnp.broadcast_to(loss_total, loss_ref.shape)
+    residual = jnp.where(is_query, jnp.exp(live_logits - log_total) - target, 0.0)
+    residual = residual.astype(jnp.bfloat16).astype(jnp.float32)
+    sym[...] = (residual + residual.T).astype(jnp.bfloat16).reshape(dp, group_rows, total_rows)
+    own_grad = (plain_product(sym[me], emb_rows) * INV_TEMP).astype(jnp.bfloat16)
+    emb_grad_ref[...] = own_grad
+    cot_g[core] = own_grad.astype(jnp.float32)[half_rows : half_rows + subs]
+    cot_copy = mp_copy(M_COT, cot_g.at[core], cot_g.at[core])
+    cot_copy.start()
+    cot_copy.wait()
+    for j in range(dp):
+        start = (j % per_core) * dq
+        cs[j] = cot_g[j // per_core, :, start : start + dq]
+    cs_args = (CS, lambda t: cs.at[t], cr)
+    dp_start(*cs_args)
+    cr[me] = cs[me]
+
+    acc_k[...] = jnp.zeros_like(acc_k)
+    acc_v[...] = jnp.zeros_like(acc_v)
+    acc_low[...] = jnp.zeros_like(acc_low)
+    local_copies[2].wait()
+    local_copies[3].wait()
+
+    def project(which):
+        @pl.loop(0, tiles)
+        def _(t):
+            cols = pl.ds(pl.multiple_of(t * TILE, TILE), TILE)
+            spot = pl.ds(pl.multiple_of(which * feats + t * TILE, TILE), TILE)
+            block = xg[which, :, cols]
+            acc_k[...] += plain_product(block, wk[spot, :])
+            acc_v[...] += plain_product(block, wv[spot, :])
+            acc_low[...] += final_product(block, down_ref[:, spot])
+
+    project(core)
+
+    dp_wait(*cs_args)
+    for j in range(dp):
+        cot_rows[j * subs : (j + 1) * subs, :] = cr[j]
+    local_copies[4].wait()
+    grad_part = final_product(cot_rows[...].astype(jnp.bfloat16), wo[...])
+    for j in range(dp):
+        part_a[j] = grad_part[j * subs : (j + 1) * subs]
+    a_args = (AP, lambda t: part_a.at[t], land_a)
+    dp_start(*a_args)
+    land_a[me] = part_a[me]
+
+    x_copy.wait()
+    project(other)
+    low = acc_low[...].astype(jnp.bfloat16)
+    low_key, low_value = low[:, :rank], low[:, rank:]
+    keys = (acc_k[...] + ADAPTER_SCALE * plain_product(low_key, kup_ref[...])).astype(jnp.bfloat16)
+    values = (acc_v[...] + ADAPTER_SCALE * plain_product(low_value, vup_ref[...])).astype(
+        jnp.bfloat16
+    )
+
+    heads = qw // HEAD_DIM
+    group_size = HEADS // KV_HEADS
+    score_scale = 1.0 / math.sqrt(HEAD_DIM)
+
+    def spread(flat, blocks):
+        blocks[...] = jnp.zeros_like(blocks)
+        for b in range(subs):
+            for h in range(heads):
+                kv = h // group_size * HEAD_DIM
+                blocks[b * heads + h : b * heads + h + 1, kv : kv + HEAD_DIM] = flat[
+                    b : b + 1, h * HEAD_DIM : (h + 1) * HEAD_DIM
+                ]
+
+    def summed(landing):
+        total = landing[0]
+        for j in range(1, dp):
+            total = total + landing[j]
+        return total.astype(jnp.bfloat16).astype(jnp.float32)
+
+    dp_wait(*q_args)
+    query_f[...] = summed(land_q)
+    spread(query_f, q_blk)
+    q_half = q_blk[...].astype(jnp.bfloat16)
+    raw = final_product(q_half, keys) * score_scale
+    head_rows = lax.broadcasted_iota(jnp.int32, raw.shape, 0)
+    token_ids = lax.broadcasted_iota(jnp.int32, raw.shape, 1)
+    live = jnp.zeros(raw.shape, jnp.bool_)
+    for b in range(subs):
+        mine = (head_rows >= b * heads) & (head_rows < (b + 1) * heads)
+        live = live | (mine & (token_ids >= b * seq_len) & (token_ids <= last[b]))
+    raw = jnp.where(live, raw, -jnp.inf)
+    weights = jnp.exp(raw - jnp.max(raw, axis=1, keepdims=True))
+    probs = weights / jnp.sum(weights, axis=1, keepdims=True)
+    dp_wait(*a_args)
+    grad_f[...] = summed(land_a)
+    spread(grad_f, g_blk)
+    g_half = g_blk[...].astype(jnp.bfloat16)
+    prob_grad = final_product(g_half, values)
+    score_grad = (
+        probs * (prob_grad - jnp.sum(probs * prob_grad, axis=1, keepdims=True)) * score_scale
+    ).astype(jnp.bfloat16)
+    query_delta = plain_product(score_grad, keys).astype(jnp.bfloat16).astype(jnp.float32)
+    for b in range(subs):
+        for h in range(heads):
+            kv = h // group_size * HEAD_DIM
+            qd_own[b : b + 1, h * HEAD_DIM : (h + 1) * HEAD_DIM] = query_delta[
+                b * heads + h : b * heads + h + 1, kv : kv + HEAD_DIM
+            ]
+    qd_args = (QD, lambda t: qd_own, qd_all)
+    dp_start(*qd_args)
+    qd_all[me] = qd_own[...]
+    key_delta = first_product(score_grad, q_half).astype(jnp.bfloat16)
+    value_delta = first_product(probs.astype(jnp.bfloat16), g_half).astype(jnp.bfloat16)
+    coef = jnp.concatenate(
+        [final_product(key_delta, kup_ref[...]), final_product(value_delta, vup_ref[...])], axis=1
+    ).astype(jnp.bfloat16)
+    coef_g[core] = coef
+    coef_copy = mp_copy(M_COEF, coef_g.at[core], coef_g.at[core])
+    coef_copy.start()
+
+    key_up = ADAPTER_SCALE * first_product(low_key, key_delta)
+    value_up = ADAPTER_SCALE * first_product(low_value, value_delta)
+    up_rows = 2 * rank // dp
+    for j in range(dp):
+        spot = j * up_rows
+        up[j] = key_up[spot : spot + up_rows] if spot < rank else value_up[
+            spot - rank : spot - rank + up_rows
+        ]
+    up_args = (UP, lambda t: up.at[t], up_land)
+    dp_start(*up_args)
+    up_land[me] = up[me]
+
+    coef_copy.wait()
+    down_part = ADAPTER_SCALE * (
+        first_product(coef_g[0], xg[core]) + first_product(coef_g[1], xg[core])
+    )
+    down_cols = feats // dp
+    for j in range(dp):
+        dn[j] = down_part[:, j * down_cols : (j + 1) * down_cols]
+    dn_args = (DN, lambda t: dn.at[t], dn_land)
+    dp_start(*dn_args)
+    dn_land[me] = dn[me]
+
+    dp_wait(*qd_args)
+    for j in range(dp):
+        qd_rows[j * subs : (j + 1) * subs, :] = qd_all[j]
+    last_part = final_product(qd_rows[...].astype(jnp.bfloat16), wq[...])
+    for j in range(dp):
+        lp[j] = last_part[j * subs : (j + 1) * subs]
+    lp_args = (LP, lambda t: lp.at[t], lp_land)
+    dp_start(*lp_args)
+    lp_land[me] = lp[me]
+
+    def portion(which, slot):
+        @pl.loop(0, tiles)
+        def _(t):
+            cols = pl.ds(pl.multiple_of(t * TILE, TILE), TILE)
+            spot = pl.ds(pl.multiple_of(which * feats + t * TILE, TILE), TILE)
+            pacc[...] = (
+                final_product(key_delta, wk[spot, :])
+                + final_product(value_delta, wv[spot, :])
+                + ADAPTER_SCALE * plain_product(coef, down_ref[:, spot])
+            )
+            pbuf[slot, :, cols] = pacc[...].astype(jnp.bfloat16)
+            for b in range(subs):
+                last_rows_f[slot, b : b + 1, cols] = pacc[pl.ds(last[b], 1), :]
+
+    portion(other, 1)
+    part_copy = mp_copy(M_PART, pbuf.at[1], pland)
+    part_copy.start()
+
+    dp_wait(*dn_args)
+    total = dn_land[0]
+    for j in range(1, dp):
+        total = total + dn_land[j]
+    down_out[core, me] = total
+    dng_args = (DNG, lambda t: down_out.at[core, me], down_out.at[core])
+    dp_start(*dng_args)
+    dp_wait(*up_args)
+    total = up_land[0]
+    for j in range(1, dp):
+        total = total + up_land[j]
+    up_out[me] = total
+    upg_args = (UPG, lambda t: up_out.at[me], up_out)
+    dp_start(*upg_args)
+
+    portion(core, 0)
+
+    dp_wait(*lp_args)
+    for which in range(mp):
+        for j in range(per_core):
+            last_total[which, :, j * dq : (j + 1) * dq] = lp_land[which * per_core + j]
+    last_send[...] = (
+        (last_rows_f[1] + last_total[other]).astype(jnp.bfloat16).astype(jnp.float32)
+    )
+    last_copy = mp_copy(M_LAST, last_send, last_land)
+    last_copy.start()
+    dp_wait(*dng_args)
+    down_copy = mp_copy(M_DN, down_out.at[core], down_out.at[core])
+    down_copy.start()
+
+    own_last = (last_rows_f[0] + last_total[core]).astype(jnp.bfloat16).astype(jnp.float32)
+    last_copy.wait()
+    last_rows_f[0] = own_last + last_land[...] + cot_g[core]
+    part_copy.wait()
+
+    @pl.loop(0, tiles)
+    def _(t):
+        cols = pl.ds(pl.multiple_of(t * TILE, TILE), TILE)
+        both = pbuf[0, :, cols].astype(jnp.float32) + pland[:, cols].astype(jnp.float32)
+        ids = lax.broadcasted_iota(jnp.int32, both.shape, 0)
+        for b in range(subs):
+            both = jnp.where(ids == last[b], last_rows_f[0, b : b + 1, cols], both)
+        input_grad_ref[:, cols] = both.astype(jnp.bfloat16)
+
+    dp_wait(*upg_args)
+    down_copy.wait()
+
+
+def fused_local(
+    query_emb, item_emb, pair_index, hard_index, hidden_in, lengths, w_query, key_weight_matrix,
+    value_weight_matrix, w_out, key_down_matrix, key_up_matrix, value_down, value_up_matrix,
+):
+    dp, mp = lax.axis_size("dp"), lax.axis_size("mp")
+    local_rows, feats = query_emb.shape
+    subs, _, seq_len, _ = hidden_in.shape
+    rows = subs * seq_len
+    rank, kw = key_up_matrix.shape
+    dq, qw = w_query.shape
+    width = feats * mp
+    heads = qw // HEAD_DIM
+    group_rows = 2 * local_rows
+    total_rows = dp * group_rows
+    emb = jnp.concatenate([query_emb, item_emb], axis=0)
+    index = jnp.concatenate([pair_index[:, None], hard_index], axis=1)
+    index = index // local_rows * group_rows + local_rows + index % local_rows
+    index = jnp.pad(index, ((0, local_rows), (0, 128 - index.shape[1])), constant_values=-1)
+    down = jnp.concatenate([key_down_matrix.T, value_down.T], axis=0)
+    f32, bf16 = jnp.float32, jnp.bfloat16
+    vmem, hbm = pl.BlockSpec(memory_space=pltpu.VMEM), pl.BlockSpec(memory_space=pl.ANY)
+    shape = jax.ShapeDtypeStruct
+    scratch = [
+        ((dp, group_rows, feats), bf16),
+        ((dp, group_rows, 128), jnp.int32),
+        ((mp, rows, feats), bf16),
+        ((mp, subs, feats), f32),
+        ((dp, subs, dq), f32),
+        ((dp, subs, dq), f32),
+        ((dp * subs, dq), f32),
+        ((dp, subs, qw), f32),
+        ((dp, subs, qw), f32),
+        ((mp, subs, feats), f32),
+        ((dp, subs, dq), f32),
+        ((dp, subs, dq), f32),
+        ((dp * subs, dq), f32),
+        ((dp, subs, qw), f32),
+        ((dp, subs, qw), f32),
+        ((mp, total_rows, total_rows), f32),
+        ((dp, group_rows, total_rows), bf16),
+        ((dq, qw), bf16),
+        ((width, kw), bf16),
+        ((width, kw), bf16),
+        ((qw, dq), bf16),
+        ((rows, kw), f32),
+        ((rows, kw), f32),
+        ((rows, 2 * rank), f32),
+        ((subs * heads, kw), f32),
+        ((subs * heads, kw), f32),
+        ((subs, qw), f32),
+        ((subs, qw), f32),
+        ((subs, qw), f32),
+        ((dp, subs, qw), f32),
+        ((dp * subs, qw), f32),
+        ((dp, subs, dq), f32),
+        ((dp, subs, dq), f32),
+        ((mp, rows, 2 * rank), bf16),
+        ((rows, TILE), f32),
+        ((2, rows, feats), bf16),
+        ((rows, feats), bf16),
+        ((2, subs, feats), f32),
+        ((subs, feats), f32),
+        ((subs, feats), f32),
+        ((dp, 2 * rank, feats // dp), f32),
+        ((dp, 2 * rank, feats // dp), f32),
+        ((dp, 2 * rank // dp, kw), f32),
+        ((dp, 2 * rank // dp, kw), f32),
+        ((mp, subs, feats), f32),
+    ]
+    loss, emb_grad, input_grad, down_grad, up_grad = pl.pallas_call(
+        functools.partial(step_kernel, dp, mp, subs, rank),
+        out_shape=(
+            shape((8, 128), f32),
+            shape((group_rows, feats), bf16),
+            shape((rows, feats), bf16),
+            shape((mp, dp, 2 * rank, feats // dp), f32),
+            shape((dp, 2 * rank // dp, kw), f32),
+        ),
+        in_specs=[pl.BlockSpec(memory_space=pltpu.SMEM), vmem, vmem]
+        + [hbm] * 5
+        + [vmem] * 3,
+        out_specs=(vmem,) * 5,
+        scratch_shapes=[pltpu.VMEM(s, t) for s, t in scratch]
+        + [
+            pltpu.SemaphoreType.DMA((12, dp)),
+            pltpu.SemaphoreType.DMA((12, dp)),
+            pltpu.SemaphoreType.DMA((8,)),
+            pltpu.SemaphoreType.DMA((8,)),
+            pltpu.SemaphoreType.DMA((5,)),
+        ],
+        compiler_params=pltpu.CompilerParams(
+            collective_id=0, has_side_effects=True, vmem_limit_bytes=60 * 1024 * 1024
+        ),
+    )(
+        lengths[:, 0], emb, index, hidden_in.reshape(rows, feats), w_query, key_weight_matrix,
+        value_weight_matrix, w_out, down, key_up_matrix, value_up_matrix,
+    )
+    down_grad = down_grad.transpose(2, 0, 1, 3).reshape(2 * rank, width)
+    up_grad = up_grad.reshape(2 * rank, kw)
+    return (
+        loss[0, 0],
+        emb_grad[:local_rows],
+        emb_grad[local_rows:],
+        input_grad.reshape(hidden_in.shape),
+        down_grad[:rank].T,
+        down_grad[rank:].T,
+        up_grad[:rank],
+        up_grad[rank:],
+    )
+
+
 def solution(mesh):
     in_specs = (
         P("dp", "mp"),
@@ -210,4 +683,6 @@
         P(None, "mp"),
         P(None, "mp"),
     )
-    return jax.shard_map(local, mesh=mesh, in_specs=in_specs, out_specs=out_specs, check_vma=False)
+    small = mesh.shape["mp"] == 2 and mesh.shape["dp"] == 16
+    body = fused_local if small else local
+    return jax.shard_map(body, mesh=mesh, in_specs=in_specs, out_specs=out_specs, check_vma=False)

time: 715 us -> 94.5 us (0.13)
  waiting for transfers between devices: 461 us -> 0 us
  blocking collectives: 126 us -> 0 us
  matrix products: 80.3 us -> 0 us
  Pallas kernels: 0 us -> 80 us
  between operations: 17.8 us -> 0.67 us
  other arithmetic: 18.4 us -> 3.18 us
    all_gather x3 -> x0, waiting for transfers between devices: 250 us -> none  [the longest x1 182 us: local(): lax.all_gather(w_query, 'dp', axis=0, tiled=True)]
    reduce_scatter x2 -> x0, waiting for transfers between devices: 162 us -> none  [the longest x1 162 us: local(): lax.psum_scatter(first_product(residual, query_emb) * INV_TEMP, 'dp', sca...]
    dot_general x26 -> x0, matrix products: 80.3 us -> none  [the longest x9 45.5 us: final_product(): lax.dot_general(left_side, right_side, (((1,), (1,)), ((), ())), preferre...]
    pallas_call x0 -> x1, Pallas kernels: none -> 80 us  [fused_local(): pl.pallas_call(functools.partial(step_kernel, dp, mp, subs, rank), out_sh...]
    psum x2 -> x0, blocking collectives: 78.5 us -> none  [the longest x1 76.1 us: local(): lax.psum((loss_part, ADAPTER_SCALE * first_product(reduced_key, key_adapt...]
    psum x1 -> x0, waiting for transfers between devices: 48.4 us -> none  [local(): lax.psum((ADAPTER_SCALE * first_product(token_inputs, key_coefficient), A...]
    all_gather x2 -> x0, blocking collectives: 47.6 us -> none  [the longest x1 45.7 us: local(): items_all = lax.all_gather(item_emb, 'dp', axis=0, tiled=True)]
    convert_element_type x4 -> x0, other arithmetic: 7.86 us -> none  [the longest x1 4.23 us: local(): input_portion.astype(jnp.bfloat16)]
  transfers between devices with their start and end apart: 6 -> 0, of which waited for: 4 -> 0; matrix products, arithmetic and copies ran while one was open for 5% -> 0% of each run, Pallas kernels for 0% -> 0%
where the time goes in v1:
time: 94.5 us; the launch traced here: 94 us
  Pallas kernels  80 us (85%)
  local copies, waits for them, and re-layouts  10.1 us (11%)
  other arithmetic  3.18 us (3%)
    pallas_call x1, Pallas kernels, fused_local(): pl.pallas_call(functools.partial(step_kernel, dp, mp, subs, rank), out_sh...  80 us

profile of v1, /device:TPU:0, one launch (start us, length us, event | category | flops | bytes accessed | tf_op | source)
XLA Modules:
  0.0 94.0 jit_solution(17678009698876731865)
XLA Ops:
  0.6 0.7 copy.25
  1.4 0.8 copy.26
  2.1 0.1 fusion.2
  2.2 0.6 pad.4.idx_ref
  2.8 1.4 %pad_maximum_fusion.1.emb_ref = bf16[16,2048]{1,0:T(8,128)(2,1)} fusion(bf16[8,2048]{1,0:T(8,128)(2,1)} %param.15, bf16[8,2048]{1,0:T(8,128)(2,1)} %param.14), kind=kLoop, calls=%fused_computation.3 | loop fusion | flops 131072 | bytes 131072 | tf_op jit(solution)/shard_map/concatenate | solution.py:562
  4.2 1.7 %pad_maximum_fusion.down_ref = bf16[32,4096]{1,0:T(8,128)(2,1)} fusion(bf16[16,4096]{1,0:T(8,128)(2,1)} %bitcast.27, bf16[16,4096]{1,0:T(8,128)(2,1)} %bitcast.28), kind=kLoop, calls=%fused_computation.2 | loop fusion | flops 524288 | bytes 524288 | tf_op jit(solution)/shard_map/concatenate | solution.py:566
  5.9 80.0 %shard_map.197 = (f32[8,128]{1,0:T(8,128)}, bf16[16,2048]{1,0:T(8,128)(2,1)}, bf16[304,2048]{1,0:T(8,128)(2,1)}, f32[2,16,32,128]{3,2,1,0:T(8,128)}, f32[16,2,512]{2,1,0:T(2,128)}) custom-call(s32[2]{0:T(128)} %bitcast.30, bf16[16,2048]{1,0:T(8,128)(2,1)} %pad_maximum_fusion.1.emb_ref, s32[16,128]{1,0:T(8,128)} %pad.4.idx_ref, bf16[304,2048]{1,0:T(8,128)(2,1)} %bitcast.23, ...), custom_call_target="tpu_custom_call" | custom-call | tf_op jit(solution)/shard_map/pallas_call | solution.py:617
  85.9 1.2 %slice.33 = f32[1,1]{1,0:T(1,128)} slice(f32[8,128]{1,0:T(8,128)} %get-tuple-element.13), slice={[0:1], [0:1]} | slice | bytes 8 | tf_op jit(solution)/shard_map/slice | solution.py:648
  87.1 1.4 %fusion.9 = (bf16[8,2048]{1,0:T(8,128)(2,1)}, bf16[8,2048]{1,0:T(8,128)(2,1)}) fusion(bf16[16,2048]{1,0:T(8,128)(2,1)} %get-tuple-element.14), kind=kLoop, calls=%fused_computation.20 | loop fusion | bytes 131072 | tf_op jit(solution)/shard_map/slice | solution.py:650
  88.5 0.8 fusion.8
  89.3 0.6 slice.43
  89.9 0.6 slice.41
  90.6 1.1 %fusion.7 = (f32[16,2,16,128]{3,0,2,1:T(8,128)S(1)}, f32[16,2,16,128]{3,0,2,1:T(8,128)S(1)}) fusion(f32[32,2,16,128]{3,0,2,1:T(8,128)} %bitcast.26), kind=kLoop, calls=%fused_computation.18 | loop fusion | bytes 1048576 | tf_op jit(solution)/shard_map/slice | solution.py:653
  91.6 0.0 copy-start
  91.7 0.1 copy.28
  91.7 0.1 copy.27
  91.8 1.1 %bitcast_bitcast_fusion = (f32[4096,16]{0,1:T(8,128)}, f32[4096,16]{0,1:T(8,128)}) fusion(f32[2,8,32,128]{3,2,1,0:T(8,128)S(1)} %bitcast.24, f32[2,8,32,128]{3,2,1,0:T(8,128)S(1)} %bitcast.25), kind=kLoop, calls=%fused_computation | loop fusion | bytes 1048576 | tf_op jit(solution)/shard_map/transpose | solution.py:653
  92.9 0.0 copy-done
  92.9 1.0 %copy.35 = bf16[2,1,152,2048]{3,2,1,0:T(8,128)(2,1)} copy(bf16[2,1,152,2048]{3,2,1,0:T(8,128)(2,1)S(1)} %bitcast.22) | data formatting | bytes 2490368
Async XLA Ops:
  91.6 1.3 %copy-start = (bf16[304,2048]{1,0:T(8,128)(2,1)S(1)}, bf16[304,2048]{1,0:T(8,128)(2,1)}, u32[]{:S(2)}) copy-start(bf16[304,2048]{1,0:T(8,128)(2,1)} %get-tuple-element.15) | copy-start | bytes 3735556

commit v2 on v0

--- a/solution.py
+++ b/solution.py
@@ -1,8 +1,11 @@
+import functools
 import math
 
 import jax
 import jax.numpy as jnp
 from jax import lax
+from jax.experimental import pallas as pl
+from jax.experimental.pallas import tpu as pltpu
 from jax.sharding import PartitionSpec as P
 
 HEADS = 32
@@ -183,6 +186,570 @@
     )
 
 
+TILE = 512
+EMB, XS, SC, RES, QP, AP, GB, QD, LP, DN, DNG = range(11)
+M_X, M_COEF, M_PART, M_LAST, M_DN = range(5)
+
+
+def plain_product(left_side, right_side):
+    return jnp.dot(left_side, right_side, preferred_element_type=jnp.float32)
+
+
+def step_kernel(
+    dp, mp, subs, rank, names, *refs,
+):
+    r = dict(zip(names, refs, strict=True))
+    len_ref, pair_ref, hard_ref = r["lengths"], r["pair"], r["hard"]
+    q_ref, item_ref, x_hbm, kup_ref, vup_ref = r["q"], r["item"], r["x"], r["kup"], r["vup"]
+    xg, wq, wk, wv, wo, down = r["xg"], r["wq"], r["wk"], r["wv"], r["wo"], r["down"]
+    ssem, rsem, msend, mrecv, csem = r["ssem"], r["rsem"], r["msend"], r["mrecv"], r["csem"]
+    me = lax.axis_index("dp")
+    core = lax.axis_index("mp")
+    other = 1 - core
+    rows, feats = x_hbm.shape
+    seq_len = rows // subs
+    local_rows = q_ref.shape[0]
+    batch = dp * local_rows
+    dq, qw = wq.shape
+    tiles = feats // TILE
+    per_core = dp // mp
+    home = me // per_core
+    slot = lax.rem(me, per_core)
+    at_home = core == home
+    mesh_id = pl.DeviceIdType.MESH
+    f32, bf16 = jnp.float32, jnp.bfloat16
+
+    local_copies = [
+        pltpu.make_async_copy(src, dst, csem.at[i])
+        for i, (src, dst) in enumerate(
+            (
+                (x_hbm, xg.at[core]),
+                (r["wq_hbm"], wq),
+                (r["wk_hbm"], wk),
+                (r["wv_hbm"], wv),
+                (r["wo_hbm"], wo),
+                (r["kdown"], down.at[pl.ds(0, rank)]),
+                (r["vdown"], down.at[pl.ds(rank, rank)]),
+            )
+        )
+    ]
+    for copy in local_copies:
+        copy.start()
+
+    barrier = pltpu.get_barrier_semaphore()
+
+    @pl.loop(1, dp * mp)
+    def _(n):
+        flat = lax.rem(me * mp + core + n, dp * mp)
+        pl.semaphore_signal(
+            barrier, inc=1, device_id=(flat // mp, lax.rem(flat, mp)), device_id_type=mesh_id
+        )
+
+    es, emb_land = r["es"], r["emb_land"]
+    both = jnp.concatenate([q_ref[...].astype(f32), item_ref[...].astype(f32)], axis=0)
+    for c in range(per_core):
+        es[c] = both[:, c * dq : (c + 1) * dq].astype(bf16)
+    pl.semaphore_wait(barrier, dp * mp - 1)
+
+    def remote(source, landing, send, recv, target, target_core):
+        return pltpu.make_async_remote_copy(
+            src_ref=source,
+            dst_ref=landing,
+            send_sem=send,
+            recv_sem=recv,
+            device_id=(target, target_core),
+            device_id_type=mesh_id,
+        )
+
+    def slice_copy(op, n, source, landing):
+        return remote(
+            source.at[n // mp], landing.at[me], ssem.at[op, n], rsem.at[op, me],
+            core * per_core + n // mp, lax.rem(n, mp),
+        )
+
+    def is_self(n):
+        return (core * per_core + n // mp == me) & (lax.rem(n, mp) == core)
+
+    def slice_start(op, source, landing):
+        @pl.loop(0, dp)
+        def _(n):
+            @pl.when(jnp.logical_not(is_self(n)))
+            def _():
+                slice_copy(op, n, source, landing).start()
+
+        @pl.when(at_home)
+        def _():
+            landing[me] = source[slot]
+
+    def slice_wait(op, source, landing):
+        @pl.loop(0, dp)
+        def _(n):
+            @pl.when(jnp.logical_not(is_self(n)))
+            def _():
+                slice_copy(op, n, source, landing).wait_send()
+
+            @pl.when(jnp.logical_not(at_home & (n == me)))
+            def _():
+                remote(
+                    source.at[0], landing.at[n], ssem.at[op, 0], rsem.at[op, n], me, other
+                ).wait_recv()
+
+    def dp_copy(op, k, source, landing):
+        target = lax.rem(me + k, dp)
+        return remote(
+            source(target), landing.at[me], ssem.at[op, k], rsem.at[op, k], target, core
+        )
+
+    def dp_start(op, source, landing):
+        @pl.loop(1, dp)
+        def _(k):
+            dp_copy(op, k, source, landing).start()
+
+    def dp_wait(op, source, landing):
+        @pl.loop(1, dp)
+        def _(k):
+            dp_copy(op, k, source, landing).wait()
+
+    def mp_copy(op, source, landing):
+        return remote(source, landing, msend.at[op], mrecv.at[op], me, other)
+
+    def total_of(landing):
+        total = landing[0]
+        for j in range(1, dp):
+            total = total + landing[j]
+        return total
+
+    emb_args = (EMB, es, emb_land)
+    slice_start(*emb_args)
+
+    local_copies[0].wait()
+    last = [jnp.clip(len_ref[b] - 1, 0, seq_len - 1) + b * seq_len for b in range(subs)]
+    one_row = lax.broadcasted_iota(jnp.int32, (8, rows), 0)
+    one_col = lax.broadcasted_iota(jnp.int32, (8, rows), 1)
+    picked_rows = jnp.zeros((8, rows), f32)
+    for b in range(subs):
+        picked_rows = jnp.where((one_row == b) & (one_col == last[b]), 1.0, picked_rows)
+    last_tokens = plain_product(picked_rows.astype(bf16), xg[core])[:subs]
+    xs, x_land = r["xs"], r["x_land"]
+    for c in range(per_core):
+        xs[c] = last_tokens[:, c * dq : (c + 1) * dq]
+    xs_args = (XS, xs, x_land)
+    slice_start(*xs_args)
+    x_copy = mp_copy(M_X, xg.at[core], xg.at[core])
+    x_copy.start()
+
+    slice_wait(*emb_args)
+    emb = emb_land[...].astype(f32)
+    queries = emb[:, :local_rows].reshape(batch, dq).astype(bf16)
+    items = emb[:, local_rows:].reshape(batch, dq).astype(bf16)
+    sc, sc_land = r["sc"], r["sc_land"]
+    sc[...] = final_product(queries, items).reshape(dp, local_rows, batch)
+    sc_args = (SC, lambda t: sc.at[t], sc_land)
+    dp_start(*sc_args)
+    sc_land[me] = sc[me]
+
+    slice_wait(*xs_args)
+    x_rows = r["x_rows"]
+    for j in range(dp):
+        x_rows[j * subs : (j + 1) * subs, :] = x_land[j]
+    local_copies[1].wait()
+    part_q, land_q = r["part_q"], r["land_q"]
+    query_part = plain_product(x_rows[...].astype(bf16), wq[...])
+    for j in range(dp):
+        part_q[j] = query_part[j * subs : (j + 1) * subs]
+
+    columns = lax.broadcasted_iota(jnp.int32, (local_rows, batch), 1)
+    row_ids = lax.broadcasted_iota(jnp.int32, (local_rows, batch), 0)
+    hard_count = jnp.zeros((local_rows, batch), f32)
+    target = jnp.zeros((local_rows, batch), f32)
+    for i in range(local_rows):
+        for h in range(hard_ref.shape[0]):
+            hit = (row_ids == i) & (columns == hard_ref[h, i])
+            hard_count = hard_count + jnp.where(hit, 1.0, 0.0)
+        target = jnp.where((row_ids == i) & (columns == pair_ref[i]), 1.0, target)
+    dp_wait(*sc_args)
+    logits = total_of(sc_land) * INV_TEMP + HARD_NEGATIVE_ADD * hard_count
+    row_top = jnp.max(logits, axis=1, keepdims=True)
+    log_total = row_top + jnp.log(jnp.sum(jnp.exp(logits - row_top), axis=1, keepdims=True))
+    picked = jnp.sum(target * logits, axis=1, keepdims=True)
+    loss_part = jnp.sum(log_total - picked, axis=0, keepdims=True)
+    residual = (jnp.exp(logits - log_total) - target).astype(bf16).astype(f32)
+    res_own, res_land = r["res_own"], r["res_land"]
+    res_own[...] = residual
+    res_args = (RES, lambda t: res_own, res_land)
+    dp_start(*res_args)
+    res_land[me] = residual
+    q_args = (QP, lambda t: part_q.at[t], land_q)
+    dp_start(*q_args)
+    land_q[me] = part_q[me]
+
+    acc_k, acc_v, acc_low = r["acc_k"], r["acc_v"], r["acc_low"]
+    acc_k[...] = jnp.zeros_like(acc_k)
+    acc_v[...] = jnp.zeros_like(acc_v)
+    acc_low[...] = jnp.zeros_like(acc_low)
+    for i in (2, 3, 5, 6):
+        local_copies[i].wait()
+
+    def project(which):
+        @pl.loop(0, tiles)
+        def _(t):
+            cols = pl.ds(pl.multiple_of(t * TILE, TILE), TILE)
+            spot = pl.ds(pl.multiple_of(which * feats + t * TILE, TILE), TILE)
+            block = xg[which, :, cols]
+            acc_k[...] += plain_product(block, wk[spot, :])
+            acc_v[...] += plain_product(block, wv[spot, :])
+            acc_low[...] += final_product(block, down[:, spot])
+
+    project(core)
+
+    dp_wait(*res_args)
+    res = res_land[...].reshape(batch, batch)
+    query_grad = plain_product(res.astype(bf16), items) * INV_TEMP
+    item_grad = (plain_product(res.T.astype(bf16), queries) * INV_TEMP).astype(bf16).astype(f32)
+    item_slabs = item_grad.reshape(dp, local_rows, dq)
+    cot_rows = r["cot_rows"]
+    for j in range(dp):
+        cot_rows[j * subs : (j + 1) * subs, :] = item_slabs[j, :subs]
+    local_copies[4].wait()
+    part_a, land_a = r["part_a"], r["land_a"]
+    grad_part = final_product(cot_rows[...].astype(bf16), wo[...])
+    for j in range(dp):
+        part_a[j] = grad_part[j * subs : (j + 1) * subs]
+    a_args = (AP, lambda t: part_a.at[t], land_a)
+    dp_start(*a_args)
+    land_a[me] = part_a[me]
+    gs, g_land = r["gs"], r["g_land"]
+    gs[...] = jnp.concatenate(
+        [query_grad.reshape(dp, local_rows, dq), item_slabs], axis=1
+    ).astype(bf16)
+
+    def back_copy(k):
+        to = lax.rem(me + k, dp)
+        return remote(gs.at[to], g_land.at[slot], ssem.at[GB, k], rsem.at[GB, slot], to, core)
+
+    @pl.when(at_home)
+    def _():
+        @pl.loop(1, dp)
+        def _(k):
+            back_copy(k).start()
+
+        g_land[slot] = gs[me]
+
+    x_copy.wait()
+    project(other)
+    low = acc_low[...].astype(bf16)
+    low_key, low_value = low[:, :rank], low[:, rank:]
+    keys = (acc_k[...] + ADAPTER_SCALE * plain_product(low_key, kup_ref[...])).astype(bf16)
+    values = (acc_v[...] + ADAPTER_SCALE * plain_product(low_value, vup_ref[...])).astype(bf16)
+
+    heads = qw // HEAD_DIM
+    group_size = HEADS // KV_HEADS
+    score_scale = 1.0 / math.sqrt(HEAD_DIM)
+
+    def spread(flat, blocks):
+        blocks[...] = jnp.zeros_like(blocks)
+        for b in range(subs):
+            for h in range(heads):
+                kv = h // group_size * HEAD_DIM
+                blocks[b * heads + h : b * heads + h + 1, kv : kv + HEAD_DIM] = flat[
+                    b : b + 1, h * HEAD_DIM : (h + 1) * HEAD_DIM
+                ]
+        return blocks[...].astype(bf16)
+
+    dp_wait(*q_args)
+    r["flat_q"][...] = total_of(land_q).astype(bf16).astype(f32)
+    q_half = spread(r["flat_q"], r["q_blk"])
+    raw = final_product(q_half, keys) * score_scale
+    head_rows = lax.broadcasted_iota(jnp.int32, raw.shape, 0)
+    token_ids = lax.broadcasted_iota(jnp.int32, raw.shape, 1)
+    live = jnp.zeros(raw.shape, jnp.bool_)
+    for b in range(subs):
+        mine = (head_rows >= b * heads) & (head_rows < (b + 1) * heads)
+        live = live | (mine & (token_ids >= b * seq_len) & (token_ids <= last[b]))
+    raw = jnp.where(live, raw, -jnp.inf)
+    weights = jnp.exp(raw - jnp.max(raw, axis=1, keepdims=True))
+    probs = weights / jnp.sum(weights, axis=1, keepdims=True)
+    dp_wait(*a_args)
+    r["flat_a"][...] = total_of(land_a).astype(bf16).astype(f32)
+    g_half = spread(r["flat_a"], r["g_blk"])
+    prob_grad = final_product(g_half, values)
+    score_grad = (
+        probs * (prob_grad - jnp.sum(probs * prob_grad, axis=1, keepdims=True)) * score_scale
+    ).astype(bf16)
+
+    query_delta = plain_product(score_grad, keys)
+    qd_f, qd_own, qd_all = r["qd_f"], r["qd_own"], r["qd_all"]
+    blocks = qw // dq
+    in_block = dq // HEAD_DIM
+    for b in range(subs):
+        for h in range(heads):
+            kv = h // group_size * HEAD_DIM
+            spot = b * blocks + h // in_block
+            lane = h % in_block * HEAD_DIM
+            qd_f[spot : spot + 1, lane : lane + HEAD_DIM] = query_delta[
+                b * heads + h : b * heads + h + 1, kv : kv + HEAD_DIM
+            ]
+    qd_own[...] = qd_f[...].astype(bf16)
+    qd_args = (QD, lambda t: qd_own, qd_all)
+    dp_start(*qd_args)
+    qd_all[me] = qd_own[...]
+
+    key_delta = first_product(score_grad, q_half).astype(bf16)
+    value_delta = first_product(probs.astype(bf16), g_half).astype(bf16)
+    coef = jnp.concatenate(
+        [final_product(key_delta, kup_ref[...]), final_product(value_delta, vup_ref[...])], axis=1
+    ).astype(bf16)
+    coef_g = r["coef_g"]
+    coef_g[core] = coef
+    coef_copy = mp_copy(M_COEF, coef_g.at[core], coef_g.at[core])
+    coef_copy.start()
+
+    dn, dn_land, dn_all = r["dn"], r["dn_land"], r["dn_all"]
+    up_grad = ADAPTER_SCALE * jnp.concatenate(
+        [first_product(low_key, key_delta), first_product(low_value, value_delta)], axis=0
+    )
+    lane_groups = up_grad.shape[1] // 128
+    cols = feats // dp
+    own_down = first_product(coef, xg[core])
+    for j in range(dp):
+        top = j // lane_groups * 8
+        lane = j % lane_groups * 128
+        dn[j, 2 * rank :, :] = up_grad[top : top + 8, lane : lane + 128]
+    coef_copy.wait()
+    down_part = ADAPTER_SCALE * (own_down + first_product(coef_g[other], xg[core]))
+    for j in range(dp):
+        dn[j, : 2 * rank, :] = down_part[:, j * cols : (j + 1) * cols]
+    dn_args = (DN, lambda t: dn.at[t], dn_land)
+    dp_start(*dn_args)
+    dn_land[me] = dn[me]
+
+    pacc, pbuf, p_land, last_f = r["pacc"], r["pbuf"], r["p_land"], r["last_f"]
+
+    def portion(which, place):
+        @pl.loop(0, tiles)
+        def _(t):
+            cols = pl.ds(pl.multiple_of(t * TILE, TILE), TILE)
+            spot = pl.ds(pl.multiple_of(which * feats + t * TILE, TILE), TILE)
+            pacc[...] = (
+                final_product(key_delta, wk[spot, :])
+                + final_product(value_delta, wv[spot, :])
+                + ADAPTER_SCALE * plain_product(coef, down[:, spot])
+            )
+            pbuf[place, :, cols] = pacc[...].astype(bf16)
+            for b in range(subs):
+                last_f[place, b : b + 1, cols] = pacc[pl.ds(last[b], 1), :]
+
+    portion(other, 1)
+    part_copy = mp_copy(M_PART, pbuf.at[1], p_land)
+    part_copy.start()
+
+    dp_wait(*qd_args)
+    changes = qd_all[...].reshape(dp * subs * blocks, dq)
+    block_ids = lax.rem(lax.broadcasted_iota(jnp.int32, (dp * subs * blocks, dq), 0), blocks)
+    last_part = jnp.zeros((dp * subs * blocks, dq), f32)
+    for c in range(blocks):
+        term = final_product(changes, wq[:, c * dq : (c + 1) * dq])
+        last_part = jnp.where(block_ids == c, term, last_part)
+    last_part = jnp.sum(last_part.reshape(dp * subs, blocks, dq), axis=1)
+    lp, lp_land = r["lp"], r["lp_land"]
+    for j in range(dp):
+        lp[j, :subs] = last_part[j * subs : (j + 1) * subs]
+        lp[j, subs:] = jnp.broadcast_to(loss_part, (lp.shape[1] - subs, dq))
+    lp_args = (LP, lambda t: lp.at[t], lp_land)
+    dp_start(*lp_args)
+    lp_land[me] = lp[me]
+
+    dp_wait(*dn_args)
+    dn_all[core, me] = total_of(dn_land)
+    dng_args = (DNG, lambda t: dn_all.at[core, me], dn_all.at[core])
+    dp_start(*dng_args)
+
+    portion(core, 0)
+
+    @pl.when(at_home)
+    def _():
+        @pl.loop(1, dp)
+        def _(k):
+            back_copy(k).wait_send()
+
+    @pl.loop(0, per_core)
+    def _(c):
+        @pl.when(core * per_core + c != me)
+        def _():
+            remote(
+                gs.at[0], g_land.at[c], ssem.at[GB, 0], rsem.at[GB, c], me, other
+            ).wait_recv()
+
+    cot = r["cot"]
+    for c in range(per_core):
+        span = slice(c * dq, (c + 1) * dq)
+        slab = g_land[c].astype(f32)
+        r["q_grad"][:, span] = slab[:local_rows].astype(bf16)
+        r["item_grad"][:, span] = slab[local_rows:].astype(bf16)
+        cot[:, span] = slab[local_rows : local_rows + subs]
+
+    dp_wait(*lp_args)
+    last_total, last_send, last_land = r["last_total"], r["last_send"], r["last_land"]
+    loss = lp_land[0, subs : subs + 1, 0:1]
+    for j in range(1, dp):
+        loss = loss + lp_land[j, subs : subs + 1, 0:1]
+    r["loss"][...] = loss / batch
+    for which in range(mp):
+        for c in range(per_core):
+            last_total[which, :, c * dq : (c + 1) * dq] = lp_land[which * per_core + c, :subs]
+    last_send[...] = (last_f[1] + last_total[other]).astype(bf16).astype(f32)
+    last_copy = mp_copy(M_LAST, last_send, last_land)
+    last_copy.start()
+    dp_wait(*dng_args)
+    down_copy = mp_copy(M_DN, dn_all.at[core], dn_all.at[core])
+    down_copy.start()
+
+    own_last = (last_f[0] + last_total[core]).astype(bf16).astype(f32)
+    last_copy.wait()
+    last_f[0] = own_last + last_land[...] + cot[...]
+    part_copy.wait()
+
+    @pl.loop(0, tiles)
+    def _(t):
+        cols = pl.ds(pl.multiple_of(t * TILE, TILE), TILE)
+        both = pbuf[0, :, cols].astype(f32) + p_land[:, cols].astype(f32)
+        ids = lax.broadcasted_iota(jnp.int32, both.shape, 0)
+        for b in range(subs):
+            both = jnp.where(ids == last[b], last_f[0, b : b + 1, cols], both)
+        r["input_grad"][:, cols] = both.astype(bf16)
+
+    for j in range(dp):
+        top = j // lane_groups * 8
+        lane = j % lane_groups * 128
+        out = r["key_up"] if top < rank else r["value_up"]
+        out[top % rank : top % rank + 8, lane : lane + 128] = dn_all[core, j, 2 * rank :, :]
+    down_copy.wait()
+    for which in range(mp):
+        for j in range(dp):
+            span = slice(which * feats + j * cols, which * feats + (j + 1) * cols)
+            r["key_down"][:, span] = dn_all[which, j, :rank, :]
+            r["value_down"][:, span] = dn_all[which, j, rank : 2 * rank, :]
+
+
+def fused_local(
+    query_emb, item_emb, pair_index, hard_index, hidden_in, lengths, w_query, key_weight_matrix,
+    value_weight_matrix, w_out, key_down_matrix, key_up_matrix, value_down, value_up_matrix,
+):
+    dp, mp = lax.axis_size("dp"), lax.axis_size("mp")
+    local_rows, feats = query_emb.shape
+    subs, _, seq_len, _ = hidden_in.shape
+    rows = subs * seq_len
+    rank, kw = key_up_matrix.shape
+    dq, qw = w_query.shape
+    width = feats * mp
+    heads = qw // HEAD_DIM
+    batch = dp * local_rows
+    per_core = dp // mp
+    blocks = qw // dq
+    slab = 2 * rank + 8
+    f32, bf16 = jnp.float32, jnp.bfloat16
+    vmem, hbm = pl.BlockSpec(memory_space=pltpu.VMEM), pl.BlockSpec(memory_space=pl.ANY)
+    smem = pl.BlockSpec(memory_space=pltpu.SMEM)
+    inputs = {
+        "lengths": (lengths[:, 0], smem),
+        "pair": (pair_index, smem),
+        "hard": (hard_index.T, smem),
+        "q": (query_emb, vmem),
+        "item": (item_emb, vmem),
+        "x": (hidden_in.reshape(rows, feats), hbm),
+        "wq_hbm": (w_query, hbm),
+        "wk_hbm": (key_weight_matrix, hbm),
+        "wv_hbm": (value_weight_matrix, hbm),
+        "wo_hbm": (w_out, hbm),
+        "kdown": (key_down_matrix.T, hbm),
+        "vdown": (value_down.T, hbm),
+        "kup": (key_up_matrix, vmem),
+        "vup": (value_up_matrix, vmem),
+    }
+    outputs = {
+        "loss": ((1, 1), f32),
+        "q_grad": ((local_rows, feats), bf16),
+        "item_grad": ((local_rows, feats), bf16),
+        "input_grad": ((rows, feats), bf16),
+        "key_down": ((rank, width), f32),
+        "value_down": ((rank, width), f32),
+        "key_up": ((rank, kw), f32),
+        "value_up": ((rank, kw), f32),
+    }
+    scratch = {
+        "es": ((per_core, 2 * local_rows, dq), bf16),
+        "emb_land": ((dp, 2 * local_rows, dq), bf16),
+        "xs": ((per_core, subs, dq), f32),
+        "x_land": ((dp, subs, dq), f32),
+        "x_rows": ((dp * subs, dq), f32),
+        "sc": ((dp, local_rows, batch), f32),
+        "sc_land": ((dp, local_rows, batch), f32),
+        "res_own": ((local_rows, batch), f32),
+        "res_land": ((dp, local_rows, batch), f32),
+        "part_q": ((dp, subs, qw), f32),
+        "land_q": ((dp, subs, qw), f32),
+        "cot_rows": ((dp * subs, dq), f32),
+        "part_a": ((dp, subs, qw), f32),
+        "land_a": ((dp, subs, qw), f32),
+        "gs": ((dp, 2 * local_rows, dq), bf16),
+        "g_land": ((per_core, 2 * local_rows, dq), bf16),
+        "cot": ((subs, feats), f32),
+        "xg": ((mp, rows, feats), bf16),
+        "wq": ((dq, qw), bf16),
+        "wk": ((width, kw), bf16),
+        "wv": ((width, kw), bf16),
+        "wo": ((qw, dq), bf16),
+        "down": ((2 * rank, width), bf16),
+        "acc_k": ((rows, kw), f32),
+        "acc_v": ((rows, kw), f32),
+        "acc_low": ((rows, 2 * rank), f32),
+        "q_blk": ((subs * heads, kw), f32),
+        "g_blk": ((subs * heads, kw), f32),
+        "flat_q": ((subs, qw), f32),
+        "flat_a": ((subs, qw), f32),
+        "qd_f": ((subs * blocks, dq), f32),
+        "qd_own": ((subs * blocks, dq), bf16),
+        "qd_all": ((dp, subs * blocks, dq), bf16),
+        "lp": ((dp, 2 * subs, dq), f32),
+        "lp_land": ((dp, 2 * subs, dq), f32),
+        "coef_g": ((mp, rows, 2 * rank), bf16),
+        "pacc": ((rows, TILE), f32),
+        "pbuf": ((2, rows, feats), bf16),
+        "p_land": ((rows, feats), bf16),
+        "last_f": ((2, subs, feats), f32),
+        "last_total": ((mp, subs, feats), f32),
+        "last_send": ((subs, feats), f32),
+        "last_land": ((subs, feats), f32),
+        "dn": ((dp, slab, feats // dp), f32),
+        "dn_land": ((dp, slab, feats // dp), f32),
+        "dn_all": ((mp, dp, slab, feats // dp), f32),
+    }
+    sems = {"ssem": (11, dp), "rsem": (11, dp), "msend": (5,), "mrecv": (5,), "csem": (7,)}
+    names = (*inputs, *outputs, *scratch, *sems)
+    out = pl.pallas_call(
+        functools.partial(step_kernel, dp, mp, subs, rank, names),
+        out_shape=tuple(jax.ShapeDtypeStruct(s, t) for s, t in outputs.values()),
+        in_specs=[spec for _, spec in inputs.values()],
+        out_specs=(vmem,) * len(outputs),
+        scratch_shapes=[pltpu.VMEM(s, t) for s, t in scratch.values()]
+        + [pltpu.SemaphoreType.DMA(s) for s in sems.values()],
+        compiler_params=pltpu.CompilerParams(
+            collective_id=0, has_side_effects=True, vmem_limit_bytes=60 * 1024 * 1024
+        ),
+    )(*(value for value, _ in inputs.values()))
+    loss, query_grad, item_grad, input_grad, key_down, value_down_grad, key_up, value_up = out
+    return (
+        loss[0, 0],
+        query_grad,
+        item_grad,
+        input_grad.reshape(hidden_in.shape),
+        key_down.T,
+        value_down_grad.T,
+        key_up,
+        value_up,
+    )
+
+
 def solution(mesh):
     in_specs = (
         P("dp", "mp"),
@@ -210,4 +777,6 @@
         P(None, "mp"),
         P(None, "mp"),
     )
-    return jax.shard_map(local, mesh=mesh, in_specs=in_specs, out_specs=out_specs, check_vma=False)
+    small = mesh.shape["mp"] == 2 and mesh.shape["dp"] == 16
+    body = fused_local if small else local
+    return jax.shard_map(body, mesh=mesh, in_specs=in_specs, out_specs=out_specs, check_vma=False)

time: 715 us -> 70.3 us (0.10)
  waiting for transfers between devices: 461 us -> 0 us
  blocking collectives: 126 us -> 0 us
  matrix products: 80.3 us -> 0 us
  Pallas kernels: 0 us -> 59.2 us
  other arithmetic: 18.4 us -> 0 us
  between operations: 17.8 us -> 2.41 us
    all_gather x3 -> x0, waiting for transfers between devices: 250 us -> none  [the longest x1 182 us: local(): lax.all_gather(w_query, 'dp', axis=0, tiled=True)]
    reduce_scatter x2 -> x0, waiting for transfers between devices: 162 us -> none  [the longest x1 162 us: local(): lax.psum_scatter(first_product(residual, query_emb) * INV_TEMP, 'dp', sca...]
    dot_general x26 -> x0, matrix products: 80.3 us -> none  [the longest x9 45.5 us: final_product(): lax.dot_general(left_side, right_side, (((1,), (1,)), ((), ())), preferre...]
    psum x2 -> x0, blocking collectives: 78.5 us -> none  [the longest x1 76.1 us: local(): lax.psum((loss_part, ADAPTER_SCALE * first_product(reduced_key, key_adapt...]
    pallas_call x0 -> x1, Pallas kernels: none -> 59.2 us  [fused_local(): pl.pallas_call(functools.partial(step_kernel, dp, mp, subs, rank, names),...]
    psum x1 -> x0, waiting for transfers between devices: 48.4 us -> none  [local(): lax.psum((ADAPTER_SCALE * first_product(token_inputs, key_coefficient), A...]
    all_gather x2 -> x0, blocking collectives: 47.6 us -> none  [the longest x1 45.7 us: local(): items_all = lax.all_gather(item_emb, 'dp', axis=0, tiled=True)]
    convert_element_type x4 -> x0, other arithmetic: 7.86 us -> none  [the longest x1 4.23 us: local(): input_portion.astype(jnp.bfloat16)]
  transfers between devices with their start and end apart: 6 -> 0, of which waited for: 4 -> 0; matrix products, arithmetic and copies ran while one was open for 5% -> 0% of each run, Pallas kernels for 0% -> 0%
where the time goes in v2:
time: 70.3 us; the launch traced here: 69.6 us
  Pallas kernels  59.2 us (84%)
  local copies, waits for them, and re-layouts  7.92 us (11%)
  between operations  2.41 us (3%)
    pallas_call x1, Pallas kernels, fused_local(): pl.pallas_call(functools.partial(step_kernel, dp, mp, subs, rank, names),...  59.2 us
    unnamed x15, local copies, waits for them, and re-layouts  7.92 us

profile of v2, /device:TPU:0, one launch (start us, length us, event | category | flops | bytes accessed | tf_op | source)
XLA Modules:
  0.0 69.6 jit_solution(15641749006404304419)
XLA Ops:
  0.6 59.2 %shard_map.197 = (f32[1,1]{1,0:T(1,128)}, bf16[8,2048]{1,0:T(8,128)(2,1)}, bf16[8,2048]{1,0:T(8,128)(2,1)}, bf16[304,2048]{1,0:T(8,128)(2,1)}, f32[16,4096]{1,0:...) custom-call(s32[2]{0:T(128)} %bitcast.18, s32[8]{0:T(128)} %refs_1_.1, s32[4,8]{1,0:T(4,128)} %bitcast.17, ...), custom_call_target="tpu_custom_call" | custom-call | tf_op jit(solution)/shard_map/pallas_call | solution.py:729
  60.5 1.4 %copy.32 = bf16[8,2048]{1,0:T(8,128)(2,1)} copy(bf16[8,2048]{1,0:T(8,128)(2,1)} %get-tuple-element.41) | data formatting | bytes 65536
  61.9 1.4 %copy.33 = bf16[8,2048]{1,0:T(8,128)(2,1)} copy(bf16[8,2048]{1,0:T(8,128)(2,1)} %get-tuple-element.42) | data formatting | bytes 65536
  63.2 0.0 copy-start.1
  63.3 0.0 copy-start
  63.3 0.0 copy-start.3
  63.3 0.0 copy-start.2
  63.3 2.5 %copy.34 = bf16[2,1,152,2048]{3,2,1,0:T(8,128)(2,1)} copy(bf16[2,1,152,2048]{3,2,1,0:T(8,128)(2,1)} %bitcast.11) | data formatting | bytes 2490368
  65.8 0.0 copy-done.1
  65.8 0.7 %copy.35 = f32[4096,16]{0,1:T(8,128)} copy(f32[4096,16]{0,1:T(8,128)S(1)} %bitcast.14) | data formatting | bytes 524288
  66.5 0.0 copy-done
  66.5 0.7 %copy.36 = f32[4096,16]{0,1:T(8,128)} copy(f32[4096,16]{0,1:T(8,128)S(1)} %bitcast.13) | data formatting | bytes 524288
  67.2 0.0 copy-done.3
  67.2 0.6 copy.37
  67.8 0.0 copy-done.2
  67.8 0.6 copy.38
Async XLA Ops:
  63.2 2.5 %copy-start.1 = (f32[16,4096]{1,0:T(8,128)S(1)}, f32[16,4096]{1,0:T(8,128)}, u32[]{:S(2)}) copy-start(f32[16,4096]{1,0:T(8,128)} %get-tuple-element.20) | copy-start | bytes 786436
  63.3 3.2 %copy-start = (f32[16,4096]{1,0:T(8,128)S(1)}, f32[16,4096]{1,0:T(8,128)}, u32[]{:S(2)}) copy-start(f32[16,4096]{1,0:T(8,128)} %get-tuple-element.21) | copy-start | bytes 786436
  63.3 3.9 %copy-start.3 = (f32[16,512]{1,0:T(8,128)S(1)}, f32[16,512]{1,0:T(8,128)}, u32[]{:S(2)}) copy-start(f32[16,512]{1,0:T(8,128)} %get-tuple-element.46) | copy-start | bytes 98308
  63.3 4.6 %copy-start.2 = (f32[16,512]{1,0:T(8,128)S(1)}, f32[16,512]{1,0:T(8,128)}, u32[]{:S(2)}) copy-start(f32[16,512]{1,0:T(8,128)} %get-tuple-element.47) | copy-start | bytes 98308

commit v3 on v2

--- a/solution.py
+++ b/solution.py
@@ -186,7 +186,7 @@
     )
 
 
-TILE = 512
+TILE = 1024
 EMB, XS, SC, RES, QP, AP, GB, QD, LP, DN, DNG = range(11)
 M_X, M_COEF, M_PART, M_LAST, M_DN = range(5)
 
@@ -201,7 +201,7 @@
     r = dict(zip(names, refs, strict=True))
     len_ref, pair_ref, hard_ref = r["lengths"], r["pair"], r["hard"]
     q_ref, item_ref, x_hbm, kup_ref, vup_ref = r["q"], r["item"], r["x"], r["kup"], r["vup"]
-    xg, wq, wk, wv, wo, down = r["xg"], r["wq"], r["wk"], r["wv"], r["wo"], r["down"]
+    xg, wq, wkv, wo, down = r["xg"], r["wq"], r["wkv"], r["wo"], r["down"]
     ssem, rsem, msend, mrecv, csem = r["ssem"], r["rsem"], r["msend"], r["mrecv"], r["csem"]
     me = lax.axis_index("dp")
     core = lax.axis_index("mp")
@@ -211,6 +211,7 @@
     local_rows = q_ref.shape[0]
     batch = dp * local_rows
     dq, qw = wq.shape
+    kw = wkv.shape[1] // 2
     tiles = feats // TILE
     per_core = dp // mp
     home = me // per_core
@@ -225,8 +226,8 @@
             (
                 (x_hbm, xg.at[core]),
                 (r["wq_hbm"], wq),
-                (r["wk_hbm"], wk),
-                (r["wv_hbm"], wv),
+                (r["wk_hbm"], wkv.at[:, pl.ds(0, kw)]),
+                (r["wv_hbm"], wkv.at[:, pl.ds(kw, kw)]),
                 (r["wo_hbm"], wo),
                 (r["kdown"], down.at[pl.ds(0, rank)]),
                 (r["vdown"], down.at[pl.ds(rank, rank)]),
@@ -263,7 +264,7 @@
 
     def slice_copy(op, n, source, landing):
         return remote(
-            source.at[n // mp], landing.at[me], ssem.at[op, n], rsem.at[op, me],
+            source.at[n // mp], landing.at[me], ssem.at[op], rsem.at[op],
             core * per_core + n // mp, lax.rem(n, mp),
         )
 
@@ -281,42 +282,44 @@
         def _():
             landing[me] = source[slot]
 
-    def slice_wait(op, source, landing):
-        @pl.loop(0, dp)
-        def _(n):
-            @pl.when(jnp.logical_not(is_self(n)))
-            def _():
-                slice_copy(op, n, source, landing).wait_send()
-
-            @pl.when(jnp.logical_not(at_home & (n == me)))
-            def _():
-                remote(
-                    source.at[0], landing.at[n], ssem.at[op, 0], rsem.at[op, n], me, other
-                ).wait_recv()
+    def arrived(op, landing, count):
+        some = landing.at[pl.ds(0, count)]
+        remote(some, some, ssem.at[op], rsem.at[op], me, other).wait_recv()
+
+    def departed(op, landing, count):
+        some = landing.at[pl.ds(0, count)]
+        remote(some, some, ssem.at[op], rsem.at[op], me, other).wait_send()
+
+    def by_home(wait, op, landing, count):
+        @pl.when(at_home)
+        def _():
+            wait(op, landing, count - 1)
+
+        @pl.when(jnp.logical_not(at_home))
+        def _():
+            wait(op, landing, count)
 
     def dp_copy(op, k, source, landing):
         target = lax.rem(me + k, dp)
         return remote(
-            source(target), landing.at[me], ssem.at[op, k], rsem.at[op, k], target, core
+            source(target), landing.at[me], ssem.at[op], rsem.at[op], target, core
         )
 
     def dp_start(op, source, landing):
-        @pl.loop(1, dp)
+        @pl.loop(1, dp, unroll=True)
         def _(k):
             dp_copy(op, k, source, landing).start()
 
     def dp_wait(op, source, landing):
-        @pl.loop(1, dp)
-        def _(k):
-            dp_copy(op, k, source, landing).wait()
+        arrived(op, landing, dp - 1)
 
     def mp_copy(op, source, landing):
         return remote(source, landing, msend.at[op], mrecv.at[op], me, other)
 
     def total_of(landing):
-        total = landing[0]
+        total = landing[0].astype(f32)
         for j in range(1, dp):
-            total = total + landing[j]
+            total = total + landing[j].astype(f32)
         return total
 
     emb_args = (EMB, es, emb_land)
@@ -338,7 +341,7 @@
     x_copy = mp_copy(M_X, xg.at[core], xg.at[core])
     x_copy.start()
 
-    slice_wait(*emb_args)
+    by_home(arrived, EMB, emb_land, dp)
     emb = emb_land[...].astype(f32)
     queries = emb[:, :local_rows].reshape(batch, dq).astype(bf16)
     items = emb[:, local_rows:].reshape(batch, dq).astype(bf16)
@@ -348,7 +351,7 @@
     dp_start(*sc_args)
     sc_land[me] = sc[me]
 
-    slice_wait(*xs_args)
+    by_home(arrived, XS, x_land, dp)
     x_rows = r["x_rows"]
     for j in range(dp):
         x_rows[j * subs : (j + 1) * subs, :] = x_land[j]
@@ -383,24 +386,16 @@
     dp_start(*q_args)
     land_q[me] = part_q[me]
 
-    acc_k, acc_v, acc_low = r["acc_k"], r["acc_v"], r["acc_low"]
-    acc_k[...] = jnp.zeros_like(acc_k)
-    acc_v[...] = jnp.zeros_like(acc_v)
-    acc_low[...] = jnp.zeros_like(acc_low)
     for i in (2, 3, 5, 6):
         local_copies[i].wait()
 
     def project(which):
-        @pl.loop(0, tiles)
-        def _(t):
-            cols = pl.ds(pl.multiple_of(t * TILE, TILE), TILE)
-            spot = pl.ds(pl.multiple_of(which * feats + t * TILE, TILE), TILE)
-            block = xg[which, :, cols]
-            acc_k[...] += plain_product(block, wk[spot, :])
-            acc_v[...] += plain_product(block, wv[spot, :])
-            acc_low[...] += final_product(block, down[:, spot])
-
-    project(core)
+        spot = pl.ds(pl.multiple_of(which * feats, feats), feats)
+        block = xg[which]
+        return plain_product(block, wkv[spot, :]), final_product(block, down[:, spot])
+
+    acc, acc_low = r["acc"], r["acc_low"]
+    acc[...], acc_low[...] = project(core)
 
     dp_wait(*res_args)
     res = res_land[...].reshape(batch, batch)
@@ -425,7 +420,7 @@
 
     def back_copy(k):
         to = lax.rem(me + k, dp)
-        return remote(gs.at[to], g_land.at[slot], ssem.at[GB, k], rsem.at[GB, slot], to, core)
+        return remote(gs.at[to], g_land.at[slot], ssem.at[GB], rsem.at[GB], to, core)
 
     @pl.when(at_home)
     def _():
@@ -436,11 +431,12 @@
         g_land[slot] = gs[me]
 
     x_copy.wait()
-    project(other)
-    low = acc_low[...].astype(bf16)
+    more, more_low = project(other)
+    low = (acc_low[...] + more_low).astype(bf16)
     low_key, low_value = low[:, :rank], low[:, rank:]
-    keys = (acc_k[...] + ADAPTER_SCALE * plain_product(low_key, kup_ref[...])).astype(bf16)
-    values = (acc_v[...] + ADAPTER_SCALE * plain_product(low_value, vup_ref[...])).astype(bf16)
+    key_part, value_part = acc[:, :kw] + more[:, :kw], acc[:, kw:] + more[:, kw:]
+    keys = (key_part + ADAPTER_SCALE * plain_product(low_key, kup_ref[...])).astype(bf16)
+    values = (value_part + ADAPTER_SCALE * plain_product(low_value, vup_ref[...])).astype(bf16)
 
     heads = qw // HEAD_DIM
     group_size = HEADS // KV_HEADS
@@ -477,6 +473,16 @@
         probs * (prob_grad - jnp.sum(probs * prob_grad, axis=1, keepdims=True)) * score_scale
     ).astype(bf16)
 
+    key_delta = first_product(score_grad, q_half).astype(bf16)
+    value_delta = first_product(probs.astype(bf16), g_half).astype(bf16)
+    coef = jnp.concatenate(
+        [final_product(key_delta, kup_ref[...]), final_product(value_delta, vup_ref[...])], axis=1
+    ).astype(bf16)
+    coef_g = r["coef_g"]
+    coef_g[core] = coef
+    coef_copy = mp_copy(M_COEF, coef_g.at[core], coef_g.at[core])
+    coef_copy.start()
+
     query_delta = plain_product(score_grad, keys)
     qd_f, qd_own, qd_all = r["qd_f"], r["qd_own"], r["qd_all"]
     blocks = qw // dq
@@ -494,16 +500,6 @@
     dp_start(*qd_args)
     qd_all[me] = qd_own[...]
 
-    key_delta = first_product(score_grad, q_half).astype(bf16)
-    value_delta = first_product(probs.astype(bf16), g_half).astype(bf16)
-    coef = jnp.concatenate(
-        [final_product(key_delta, kup_ref[...]), final_product(value_delta, vup_ref[...])], axis=1
-    ).astype(bf16)
-    coef_g = r["coef_g"]
-    coef_g[core] = coef
-    coef_copy = mp_copy(M_COEF, coef_g.at[core], coef_g.at[core])
-    coef_copy.start()
-
     dn, dn_land, dn_all = r["dn"], r["dn_land"], r["dn_all"]
     up_grad = ADAPTER_SCALE * jnp.concatenate(
         [first_product(low_key, key_delta), first_product(low_value, value_delta)], axis=0
@@ -514,33 +510,36 @@
     for j in range(dp):
         top = j // lane_groups * 8
         lane = j % lane_groups * 128
-        dn[j, 2 * rank :, :] = up_grad[top : top + 8, lane : lane + 128]
+        up_slab = up_grad[top : top + 8, lane : lane + 128]
+        dn[j, 2 * rank :, :] = jnp.concatenate([up_slab, jnp.zeros_like(up_slab)], 0).astype(bf16)
     coef_copy.wait()
     down_part = ADAPTER_SCALE * (own_down + first_product(coef_g[other], xg[core]))
     for j in range(dp):
-        dn[j, : 2 * rank, :] = down_part[:, j * cols : (j + 1) * cols]
+        dn[j, : 2 * rank, :] = down_part[:, j * cols : (j + 1) * cols].astype(bf16)
     dn_args = (DN, lambda t: dn.at[t], dn_land)
     dp_start(*dn_args)
     dn_land[me] = dn[me]
 
     pacc, pbuf, p_land, last_f = r["pacc"], r["pbuf"], r["p_land"], r["last_f"]
-
-    def portion(which, place):
+    deltas = jnp.concatenate([key_delta, value_delta], axis=1)
+
+    def portion(which, place, finish):
         @pl.loop(0, tiles)
         def _(t):
             cols = pl.ds(pl.multiple_of(t * TILE, TILE), TILE)
             spot = pl.ds(pl.multiple_of(which * feats + t * TILE, TILE), TILE)
-            pacc[...] = (
-                final_product(key_delta, wk[spot, :])
-                + final_product(value_delta, wv[spot, :])
-                + ADAPTER_SCALE * plain_product(coef, down[:, spot])
+            pacc[...] = final_product(deltas, wkv[spot, :]) + ADAPTER_SCALE * plain_product(
+                coef, down[:, spot]
             )
-            pbuf[place, :, cols] = pacc[...].astype(bf16)
             for b in range(subs):
                 last_f[place, b : b + 1, cols] = pacc[pl.ds(last[b], 1), :]
-
-    portion(other, 1)
-    part_copy = mp_copy(M_PART, pbuf.at[1], p_land)
+            finish(cols, pacc[...].astype(bf16))
+
+    def to_other(cols, share):
+        pbuf[:, cols] = share
+
+    portion(other, 1, to_other)
+    part_copy = mp_copy(M_PART, pbuf, p_land)
     part_copy.start()
 
     dp_wait(*qd_args)
@@ -560,33 +559,18 @@
     lp_land[me] = lp[me]
 
     dp_wait(*dn_args)
-    dn_all[core, me] = total_of(dn_land)
+    dn_all[core, me] = total_of(dn_land).astype(bf16)
     dng_args = (DNG, lambda t: dn_all.at[core, me], dn_all.at[core])
     dp_start(*dng_args)
 
-    portion(core, 0)
-
-    @pl.when(at_home)
-    def _():
-        @pl.loop(1, dp)
-        def _(k):
-            back_copy(k).wait_send()
-
-    @pl.loop(0, per_core)
-    def _(c):
-        @pl.when(core * per_core + c != me)
-        def _():
-            remote(
-                gs.at[0], g_land.at[c], ssem.at[GB, 0], rsem.at[GB, c], me, other
-            ).wait_recv()
-
-    cot = r["cot"]
-    for c in range(per_core):
-        span = slice(c * dq, (c + 1) * dq)
-        slab = g_land[c].astype(f32)
-        r["q_grad"][:, span] = slab[:local_rows].astype(bf16)
-        r["item_grad"][:, span] = slab[local_rows:].astype(bf16)
-        cot[:, span] = slab[local_rows : local_rows + subs]
+    part_copy.wait()
+
+    def to_sum(cols, share):
+        r["input_sum"][:, cols] = (share.astype(f32) + p_land[:, cols].astype(f32)).astype(bf16)
+
+    portion(core, 0, to_sum)
+
+    by_home(arrived, GB, g_land, per_core)
 
     dp_wait(*lp_args)
     last_total, last_send, last_land = r["last_total"], r["last_send"], r["last_land"]
@@ -606,29 +590,59 @@
 
     own_last = (last_f[0] + last_total[core]).astype(bf16).astype(f32)
     last_copy.wait()
-    last_f[0] = own_last + last_land[...] + cot[...]
-    part_copy.wait()
-
-    @pl.loop(0, tiles)
-    def _(t):
-        cols = pl.ds(pl.multiple_of(t * TILE, TILE), TILE)
-        both = pbuf[0, :, cols].astype(f32) + p_land[:, cols].astype(f32)
-        ids = lax.broadcasted_iota(jnp.int32, both.shape, 0)
+    r["last_sum"][...] = own_last + last_land[...]
+    for j in range(dp):
+        r["up_all"][j] = dn_all[core, j, 2 * rank :, :]
+    down_copy.wait()
+
+    by_home(departed, EMB, emb_land, dp)
+    by_home(departed, XS, x_land, dp)
+
+    @pl.when(at_home)
+    def _():
+        departed(GB, gs, dp - 1)
+
+    for op, _, landing in (sc_args, res_args, q_args, a_args, qd_args, lp_args, dn_args, dng_args):
+        departed(op, landing, dp - 1)
+
+
+def result_kernel(
+    rank, len_ref, loss_sum, g_land, input_sum, last_sum, dn_all, up_all,
+    loss, q_grad, item_grad, input_grad, key_down, value_down, key_up, value_up,
+):
+    f32, bf16 = jnp.float32, jnp.bfloat16
+    mp, dp, _, cols = dn_all.shape
+    per_core, group_rows, dq = g_land.shape
+    local_rows = group_rows // 2
+    subs, feats = last_sum.shape
+    rows = input_sum.shape[0]
+    seq_len = rows // subs
+    loss[...] = loss_sum[...]
+    ids = lax.broadcasted_iota(jnp.int32, (rows, dq), 0)
+    for c in range(per_core):
+        span = slice(c * dq, (c + 1) * dq)
+        slab = g_land[c].astype(f32)
+        q_grad[:, span] = slab[:local_rows].astype(bf16)
+        item_grad[:, span] = slab[local_rows:].astype(bf16)
+        ends = last_sum[:, span] + slab[local_rows : local_rows + subs]
+        tokens = input_sum[:, span].astype(f32)
         for b in range(subs):
-            both = jnp.where(ids == last[b], last_f[0, b : b + 1, cols], both)
-        r["input_grad"][:, cols] = both.astype(bf16)
-
+            last = jnp.clip(len_ref[b] - 1, 0, seq_len - 1) + b * seq_len
+            tokens = jnp.where(ids == last, ends[b : b + 1], tokens)
+        input_grad[:, span] = tokens.astype(bf16)
+    lane_groups = key_up.shape[1] // 128
     for j in range(dp):
         top = j // lane_groups * 8
         lane = j % lane_groups * 128
-        out = r["key_up"] if top < rank else r["value_up"]
-        out[top % rank : top % rank + 8, lane : lane + 128] = dn_all[core, j, 2 * rank :, :]
-    down_copy.wait()
+        out = key_up if top < rank else value_up
+        slab = up_all[j].astype(f32)
+        out[top % rank : top % rank + 8, lane : lane + 128] = slab[:8]
     for which in range(mp):
         for j in range(dp):
             span = slice(which * feats + j * cols, which * feats + (j + 1) * cols)
-            r["key_down"][:, span] = dn_all[which, j, :rank, :]
-            r["value_down"][:, span] = dn_all[which, j, rank : 2 * rank, :]
+            slab = dn_all[which, j, : 2 * rank, :].astype(f32)
+            key_down[:, span] = slab[:rank]
+            value_down[:, span] = slab[rank:]
 
 
 def fused_local(
@@ -646,7 +660,7 @@
     batch = dp * local_rows
     per_core = dp // mp
     blocks = qw // dq
-    slab = 2 * rank + 8
+    slab = 2 * rank + 16
     f32, bf16 = jnp.float32, jnp.bfloat16
     vmem, hbm = pl.BlockSpec(memory_space=pltpu.VMEM), pl.BlockSpec(memory_space=pl.ANY)
     smem = pl.BlockSpec(memory_space=pltpu.SMEM)
@@ -666,16 +680,24 @@
         "kup": (key_up_matrix, vmem),
         "vup": (value_up_matrix, vmem),
     }
-    outputs = {
+    middle = {
         "loss": ((1, 1), f32),
-        "q_grad": ((local_rows, feats), bf16),
-        "item_grad": ((local_rows, feats), bf16),
-        "input_grad": ((rows, feats), bf16),
-        "key_down": ((rank, width), f32),
-        "value_down": ((rank, width), f32),
-        "key_up": ((rank, kw), f32),
-        "value_up": ((rank, kw), f32),
+        "g_land": ((per_core, 2 * local_rows, dq), bf16),
+        "input_sum": ((rows, feats), bf16),
+        "last_sum": ((subs, feats), f32),
+        "dn_all": ((mp, dp, slab, feats // dp), bf16),
+        "up_all": ((dp, 16, 128), bf16),
     }
+    outputs = (
+        ((1, 1), f32),
+        ((local_rows, feats), bf16),
+        ((local_rows, feats), bf16),
+        ((rows, feats), bf16),
+        ((rank, width), f32),
+        ((rank, width), f32),
+        ((rank, kw), f32),
+        ((rank, kw), f32),
+    )
     scratch = {
         "es": ((per_core, 2 * local_rows, dq), bf16),
         "emb_land": ((dp, 2 * local_rows, dq), bf16),
@@ -692,16 +714,12 @@
         "part_a": ((dp, subs, qw), f32),
         "land_a": ((dp, subs, qw), f32),
         "gs": ((dp, 2 * local_rows, dq), bf16),
-        "g_land": ((per_core, 2 * local_rows, dq), bf16),
-        "cot": ((subs, feats), f32),
         "xg": ((mp, rows, feats), bf16),
         "wq": ((dq, qw), bf16),
-        "wk": ((width, kw), bf16),
-        "wv": ((width, kw), bf16),
+        "wkv": ((width, 2 * kw), bf16),
         "wo": ((qw, dq), bf16),
         "down": ((2 * rank, width), bf16),
-        "acc_k": ((rows, kw), f32),
-        "acc_v": ((rows, kw), f32),
+        "acc": ((rows, 2 * kw), f32),
         "acc_low": ((rows, 2 * rank), f32),
         "q_blk": ((subs * heads, kw), f32),
         "g_blk": ((subs * heads, kw), f32),
@@ -714,29 +732,35 @@
         "lp_land": ((dp, 2 * subs, dq), f32),
         "coef_g": ((mp, rows, 2 * rank), bf16),
         "pacc": ((rows, TILE), f32),
-        "pbuf": ((2, rows, feats), bf16),
+        "pbuf": ((rows, feats), bf16),
         "p_land": ((rows, feats), bf16),
         "last_f": ((2, subs, feats), f32),
         "last_total": ((mp, subs, feats), f32),
         "last_send": ((subs, feats), f32),
         "last_land": ((subs, feats), f32),
-        "dn": ((dp, slab, feats // dp), f32),
-        "dn_land": ((dp, slab, feats // dp), f32),
-        "dn_all": ((mp, dp, slab, feats // dp), f32),
+        "dn": ((dp, slab, feats // dp), bf16),
+        "dn_land": ((dp, slab, feats // dp), bf16),
     }
-    sems = {"ssem": (11, dp), "rsem": (11, dp), "msend": (5,), "mrecv": (5,), "csem": (7,)}
-    names = (*inputs, *outputs, *scratch, *sems)
-    out = pl.pallas_call(
+    sems = {"ssem": (11,), "rsem": (11,), "msend": (5,), "mrecv": (5,), "csem": (7,)}
+    names = (*inputs, *middle, *scratch, *sems)
+    parts = pl.pallas_call(
         functools.partial(step_kernel, dp, mp, subs, rank, names),
-        out_shape=tuple(jax.ShapeDtypeStruct(s, t) for s, t in outputs.values()),
+        out_shape=tuple(jax.ShapeDtypeStruct(s, t) for s, t in middle.values()),
         in_specs=[spec for _, spec in inputs.values()],
-        out_specs=(vmem,) * len(outputs),
+        out_specs=(vmem,) * len(middle),
         scratch_shapes=[pltpu.VMEM(s, t) for s, t in scratch.values()]
         + [pltpu.SemaphoreType.DMA(s) for s in sems.values()],
         compiler_params=pltpu.CompilerParams(
             collective_id=0, has_side_effects=True, vmem_limit_bytes=60 * 1024 * 1024
         ),
     )(*(value for value, _ in inputs.values()))
+    out = pl.pallas_call(
+        functools.partial(result_kernel, rank),
+        out_shape=tuple(jax.ShapeDtypeStruct(s, t) for s, t in outputs),
+        in_specs=[smem] + [vmem] * len(middle),
+        out_specs=(vmem,) * len(outputs),
+        compiler_params=pltpu.CompilerParams(vmem_limit_bytes=32 * 1024 * 1024),
+    )(lengths[:, 0], *parts)
     loss, query_grad, item_grad, input_grad, key_down, value_down_grad, key_up, value_up = out
     return (
         loss[0, 0],

time: 70.3 us -> 61.5 us (0.87)
  Pallas kernels: 59.2 us -> 55.7 us
  local copies, waits for them, and re-layouts: 7.92 us -> 4.68 us
  between operations: 2.41 us -> 0.68 us
    pallas_call x1, Pallas kernels: 59.2 us -> 52.9 us  [fused_local(): pl.pallas_call(functools.partial(step_kernel, dp, mp, subs, rank, names),...]
    unnamed x15 -> x12, local copies, waits for them, and re-layouts: 7.92 us -> 4.68 us
    pallas_call x0 -> x1, Pallas kernels: none -> 2.82 us  [fused_local(): pl.pallas_call(functools.partial(result_kernel, rank), out_shape=tuple((j...]
where the time goes in v3:
time: 61.5 us; the launch traced here: 61 us
  Pallas kernels  55.7 us (91%)
  local copies, waits for them, and re-layouts  4.68 us (8%)
  between operations  0.68 us (1%)
    pallas_call x1, Pallas kernels, fused_local(): pl.pallas_call(functools.partial(step_kernel, dp, mp, subs, rank, names),...  52.9 us
    unnamed x12, local copies, waits for them, and re-layouts  4.68 us
    pallas_call x1, Pallas kernels, fused_local(): pl.pallas_call(functools.partial(result_kernel, rank), out_shape=tuple((j...  2.82 us

profile of v3, /device:TPU:0, one launch (start us, length us, event | category | flops | bytes accessed | tf_op | source)
XLA Modules:
  0.0 61.0 jit_solution(15078042221631257388)
XLA Ops:
  0.6 0.0 copy-start.5
  0.6 52.9 %shard_map.197 = (f32[1,1]{1,0:T(1,128)}, bf16[8,16,256]{2,1,0:T(8,128)(2,1)}, bf16[304,2048]{1,0:T(8,128)(2,1)}, f32[2,2048]{1,0:T(2,128)}, bf16[2,16,48,128]{3...) custom-call(s32[2]{0:T(128)} %bitcast.11, s32[8]{0:T(128)} %refs_1_.1, s32[4,8]{1,0:T(4,128)} %bitcast.16, ...), custom_call_target="tpu_custom_call" | custom-call | tf_op jit(solution)/shard_map/pallas_call | solution.py:746
  53.5 0.0 copy-done.5
  53.5 0.0 copy-start
  53.5 1.3 %copy-done = bf16[304,2048]{1,0:T(8,128)(2,1)S(1)} copy-done((bf16[304,2048]{1,0:T(8,128)(2,1)S(1)}, bf16[304,2048]{1,0:T(8,128)(2,1)}, u32[]{:S(2)}) %copy-start) | copy-done | bytes 1245208
  54.8 0.0 copy-start.1
  54.8 1.0 %copy-done.1 = bf16[2,16,48,128]{3,2,1,0:T(8,128)(2,1)S(1)} copy-done((bf16[2,16,48,128]{3,2,1,0:T(8,128)(2,1)S(1)}, bf16[2,16,48,128]{3,2,1,0:T(8,128)(2,1)}, u32[]{:S(2)}) %copy-start.1) | copy-done | bytes 393240
  55.8 0.0 copy-start.2
  55.8 0.8 %copy-done.2 = bf16[8,16,256]{2,1,0:T(8,128)(2,1)S(1)} copy-done((bf16[8,16,256]{2,1,0:T(8,128)(2,1)S(1)}, bf16[8,16,256]{2,1,0:T(8,128)(2,1)}, u32[]{:S(2)}) %copy-start.2) | copy-done | bytes 65560
  56.7 0.0 copy-start.3
  56.7 0.8 %copy-done.3 = bf16[16,16,128]{2,1,0:T(8,128)(2,1)S(1)} copy-done((bf16[16,16,128]{2,1,0:T(8,128)(2,1)S(1)}, bf16[16,16,128]{2,1,0:T(8,128)(2,1)}, u32[]{:S(2)}) %copy-start.3) | copy-done | bytes 65560
  57.5 0.0 copy-start.4
  57.5 0.7 %copy-done.4 = f32[2,2048]{1,0:T(2,128)S(1)} copy-done((f32[2,2048]{1,0:T(2,128)S(1)}, f32[2,2048]{1,0:T(2,128)}, u32[]{:S(2)}) %copy-start.4) | copy-done | bytes 16408
  58.2 2.8 %shard_map.198 = (f32[1,1]{1,0:T(1,128)}, bf16[8,2048]{1,0:T(8,128)(2,1)}, bf16[8,2048]{1,0:T(8,128)(2,1)}, bf16[304,2048]{1,0:T(8,128)(2,1)}, f32[16,4096]{1,0:...) custom-call(s32[2]{0:T(128)S(1)} %bitcast.12, f32[1,1]{1,0:T(1,128)} %get-tuple-element.22.loss_sum, ...), custom_call_target="tpu_custom_call" | custom-call | tf_op jit(solution)/shard_map/pallas_call | solution.py:757
Async XLA Ops:
  0.6 52.9 %copy-start.5 = (s32[2,1]{0,1:T(1,128)S(1)}, s32[2,1]{0,1:T(1,128)}, u32[]{:S(2)}) copy-start(s32[2,1]{0,1:T(1,128)} %param.19) | copy-start | bytes 28
  53.5 1.3 %copy-start = (bf16[304,2048]{1,0:T(8,128)(2,1)S(1)}, bf16[304,2048]{1,0:T(8,128)(2,1)}, u32[]{:S(2)}) copy-start(bf16[304,2048]{1,0:T(8,128)(2,1)} %get-tuple-element.24.input_sum) | copy-start | bytes 3735556
  54.8 1.0 %copy-start.1 = (bf16[2,16,48,128]{3,2,1,0:T(8,128)(2,1)S(1)}, bf16[2,16,48,128]{3,2,1,0:T(8,128)(2,1)}, u32[]{:S(2)}) copy-start(bf16[2,16,48,128]{3,2,1,0:T(8,128)(2,1)} %get-tuple-element.26.dn_all) | copy-start | bytes 1179652
  55.8 0.8 %copy-start.2 = (bf16[8,16,256]{2,1,0:T(8,128)(2,1)S(1)}, bf16[8,16,256]{2,1,0:T(8,128)(2,1)}, u32[]{:S(2)}) copy-start(bf16[8,16,256]{2,1,0:T(8,128)(2,1)} %get-tuple-element.23.g_land) | copy-start | bytes 196612
  56.7 0.8 %copy-start.3 = (bf16[16,16,128]{2,1,0:T(8,128)(2,1)S(1)}, bf16[16,16,128]{2,1,0:T(8,128)(2,1)}, u32[]{:S(2)}) copy-start(bf16[16,16,128]{2,1,0:T(8,128)(2,1)} %get-tuple-element.27.up_all) | copy-start | bytes 196612
  57.5 0.7 %copy-start.4 = (f32[2,2048]{1,0:T(2,128)S(1)}, f32[2,2048]{1,0:T(2,128)}, u32[]{:S(2)}) copy-start(f32[2,2048]{1,0:T(2,128)} %get-tuple-element.25.last_sum) | copy-start | bytes 49156

commit v4 on v3

--- a/solution.py
+++ b/solution.py
@@ -187,7 +187,8 @@
 
 
 TILE = 1024
-EMB, XS, SC, RES, QP, AP, GB, QD, LP, DN, DNG = range(11)
+PLANE = 4
+EMB, XS, SC, RES, QP, QZ, AP, AZ, GB, QD, LP, DN, DZ, DNG = range(14)
 M_X, M_COEF, M_PART, M_LAST, M_DN = range(5)
 
 
@@ -318,9 +319,36 @@
 
     def total_of(landing):
         total = landing[0].astype(f32)
-        for j in range(1, dp):
+        for j in range(1, landing.shape[0]):
             total = total + landing[j].astype(f32)
         return total
+
+    spot_in_plane, level = lax.rem(me, PLANE), me // PLANE
+    levels = dp // PLANE
+
+    def plane_start(op, source, landing):
+        for k in range(1, PLANE):
+            to = lax.rem(spot_in_plane + k, PLANE)
+            remote(
+                source.at[to], landing.at[spot_in_plane], ssem.at[op], rsem.at[op],
+                level * PLANE + to, core,
+            ).start()
+        landing[spot_in_plane] = source[spot_in_plane]
+
+    def line_start(op, plane_op, plane_landing, source, landing):
+        arrived(plane_op, plane_landing, PLANE - 1)
+        source[...] = total_of(plane_landing)
+        for k in range(1, levels):
+            to = lax.rem(level + k, levels)
+            remote(
+                source.at[to], landing.at[level], ssem.at[op], rsem.at[op],
+                to * PLANE + spot_in_plane, core,
+            ).start()
+        landing[level] = source[level]
+
+    def line_total(op, landing):
+        arrived(op, landing, levels - 1)
+        return total_of(landing)
 
     emb_args = (EMB, es, emb_land)
     slice_start(*emb_args)
@@ -356,10 +384,10 @@
     for j in range(dp):
         x_rows[j * subs : (j + 1) * subs, :] = x_land[j]
     local_copies[1].wait()
-    part_q, land_q = r["part_q"], r["land_q"]
+    part_q, plane_q, line_q, land_q = r["part_q"], r["plane_q"], r["line_q"], r["land_q"]
     query_part = plain_product(x_rows[...].astype(bf16), wq[...])
     for j in range(dp):
-        part_q[j] = query_part[j * subs : (j + 1) * subs]
+        part_q[j % PLANE, j // PLANE] = query_part[j * subs : (j + 1) * subs]
 
     columns = lax.broadcasted_iota(jnp.int32, (local_rows, batch), 1)
     row_ids = lax.broadcasted_iota(jnp.int32, (local_rows, batch), 0)
@@ -382,9 +410,7 @@
     res_args = (RES, lambda t: res_own, res_land)
     dp_start(*res_args)
     res_land[me] = residual
-    q_args = (QP, lambda t: part_q.at[t], land_q)
-    dp_start(*q_args)
-    land_q[me] = part_q[me]
+    plane_start(QP, part_q, plane_q)
 
     for i in (2, 3, 5, 6):
         local_copies[i].wait()
@@ -396,6 +422,7 @@
 
     acc, acc_low = r["acc"], r["acc_low"]
     acc[...], acc_low[...] = project(core)
+    line_start(QZ, QP, plane_q, line_q, land_q)
 
     dp_wait(*res_args)
     res = res_land[...].reshape(batch, batch)
@@ -406,13 +433,11 @@
     for j in range(dp):
         cot_rows[j * subs : (j + 1) * subs, :] = item_slabs[j, :subs]
     local_copies[4].wait()
-    part_a, land_a = r["part_a"], r["land_a"]
+    part_a, plane_a, line_a, land_a = r["part_a"], r["plane_a"], r["line_a"], r["land_a"]
     grad_part = final_product(cot_rows[...].astype(bf16), wo[...])
     for j in range(dp):
-        part_a[j] = grad_part[j * subs : (j + 1) * subs]
-    a_args = (AP, lambda t: part_a.at[t], land_a)
-    dp_start(*a_args)
-    land_a[me] = part_a[me]
+        part_a[j % PLANE, j // PLANE] = grad_part[j * subs : (j + 1) * subs]
+    plane_start(AP, part_a, plane_a)
     gs, g_land = r["gs"], r["g_land"]
     gs[...] = jnp.concatenate(
         [query_grad.reshape(dp, local_rows, dq), item_slabs], axis=1
@@ -432,6 +457,7 @@
 
     x_copy.wait()
     more, more_low = project(other)
+    line_start(AZ, AP, plane_a, line_a, land_a)
     low = (acc_low[...] + more_low).astype(bf16)
     low_key, low_value = low[:, :rank], low[:, rank:]
     key_part, value_part = acc[:, :kw] + more[:, :kw], acc[:, kw:] + more[:, kw:]
@@ -452,8 +478,7 @@
                 ]
         return blocks[...].astype(bf16)
 
-    dp_wait(*q_args)
-    r["flat_q"][...] = total_of(land_q).astype(bf16).astype(f32)
+    r["flat_q"][...] = line_total(QZ, land_q).astype(bf16).astype(f32)
     q_half = spread(r["flat_q"], r["q_blk"])
     raw = final_product(q_half, keys) * score_scale
     head_rows = lax.broadcasted_iota(jnp.int32, raw.shape, 0)
@@ -465,8 +490,7 @@
     raw = jnp.where(live, raw, -jnp.inf)
     weights = jnp.exp(raw - jnp.max(raw, axis=1, keepdims=True))
     probs = weights / jnp.sum(weights, axis=1, keepdims=True)
-    dp_wait(*a_args)
-    r["flat_a"][...] = total_of(land_a).astype(bf16).astype(f32)
+    r["flat_a"][...] = line_total(AZ, land_a).astype(bf16).astype(f32)
     g_half = spread(r["flat_a"], r["g_blk"])
     prob_grad = final_product(g_half, values)
     score_grad = (
@@ -500,7 +524,8 @@
     dp_start(*qd_args)
     qd_all[me] = qd_own[...]
 
-    dn, dn_land, dn_all = r["dn"], r["dn_land"], r["dn_all"]
+    dn, dn_plane, dn_line, dn_land = r["dn"], r["dn_plane"], r["dn_line"], r["dn_land"]
+    dn_all = r["dn_all"]
     up_grad = ADAPTER_SCALE * jnp.concatenate(
         [first_product(low_key, key_delta), first_product(low_value, value_delta)], axis=0
     )
@@ -510,15 +535,12 @@
     for j in range(dp):
         top = j // lane_groups * 8
         lane = j % lane_groups * 128
-        up_slab = up_grad[top : top + 8, lane : lane + 128]
-        dn[j, 2 * rank :, :] = jnp.concatenate([up_slab, jnp.zeros_like(up_slab)], 0).astype(bf16)
+        dn[j % PLANE, j // PLANE, 2 * rank :, :] = up_grad[top : top + 8, lane : lane + 128]
     coef_copy.wait()
     down_part = ADAPTER_SCALE * (own_down + first_product(coef_g[other], xg[core]))
     for j in range(dp):
-        dn[j, : 2 * rank, :] = down_part[:, j * cols : (j + 1) * cols].astype(bf16)
-    dn_args = (DN, lambda t: dn.at[t], dn_land)
-    dp_start(*dn_args)
-    dn_land[me] = dn[me]
+        dn[j % PLANE, j // PLANE, : 2 * rank, :] = down_part[:, j * cols : (j + 1) * cols]
+    plane_start(DN, dn, dn_plane)
 
     pacc, pbuf, p_land, last_f = r["pacc"], r["pbuf"], r["p_land"], r["last_f"]
     deltas = jnp.concatenate([key_delta, value_delta], axis=1)
@@ -557,18 +579,20 @@
     lp_args = (LP, lambda t: lp.at[t], lp_land)
     dp_start(*lp_args)
     lp_land[me] = lp[me]
-
-    dp_wait(*dn_args)
-    dn_all[core, me] = total_of(dn_land).astype(bf16)
+    line_start(DZ, DN, dn_plane, dn_line, dn_land)
+
+    part_copy.wait()
+
+    def to_sum(cols, share):
+        r["input_sum"][:, cols] = (share.astype(f32) + p_land[:, cols].astype(f32)).astype(bf16)
+
+    portion(core, 0, to_sum)
+
+    dn_sum = line_total(DZ, dn_land)
+    dn_all[core, me] = jnp.concatenate([dn_sum, jnp.zeros((8, cols), f32)], 0).astype(bf16)
     dng_args = (DNG, lambda t: dn_all.at[core, me], dn_all.at[core])
     dp_start(*dng_args)
 
-    part_copy.wait()
-
-    def to_sum(cols, share):
-        r["input_sum"][:, cols] = (share.astype(f32) + p_land[:, cols].astype(f32)).astype(bf16)
-
-    portion(core, 0, to_sum)
 
     by_home(arrived, GB, g_land, per_core)
 
@@ -602,8 +626,12 @@
     def _():
         departed(GB, gs, dp - 1)
 
-    for op, _, landing in (sc_args, res_args, q_args, a_args, qd_args, lp_args, dn_args, dng_args):
+    for op, _, landing in (sc_args, res_args, qd_args, lp_args, dng_args):
         departed(op, landing, dp - 1)
+    for op, landing in ((QP, plane_q), (AP, plane_a), (DN, dn_plane)):
+        departed(op, landing, PLANE - 1)
+    for op, landing in ((QZ, land_q), (AZ, land_a), (DZ, dn_land)):
+        departed(op, landing, levels - 1)
 
 
 def result_kernel(
@@ -659,6 +687,7 @@
     heads = qw // HEAD_DIM
     batch = dp * local_rows
     per_core = dp // mp
+    levels = dp // PLANE
     blocks = qw // dq
     slab = 2 * rank + 16
     f32, bf16 = jnp.float32, jnp.bfloat16
@@ -708,11 +737,15 @@
         "sc_land": ((dp, local_rows, batch), f32),
         "res_own": ((local_rows, batch), f32),
         "res_land": ((dp, local_rows, batch), f32),
-        "part_q": ((dp, subs, qw), f32),
-        "land_q": ((dp, subs, qw), f32),
+        "part_q": ((PLANE, levels, subs, qw), f32),
+        "plane_q": ((PLANE, levels, subs, qw), f32),
+        "line_q": ((levels, subs, qw), f32),
+        "land_q": ((levels, subs, qw), f32),
         "cot_rows": ((dp * subs, dq), f32),
-        "part_a": ((dp, subs, qw), f32),
-        "land_a": ((dp, subs, qw), f32),
+        "part_a": ((PLANE, levels, subs, qw), f32),
+        "plane_a": ((PLANE, levels, subs, qw), f32),
+        "line_a": ((levels, subs, qw), f32),
+        "land_a": ((levels, subs, qw), f32),
         "gs": ((dp, 2 * local_rows, dq), bf16),
         "xg": ((mp, rows, feats), bf16),
         "wq": ((dq, qw), bf16),
@@ -738,10 +771,12 @@
         "last_total": ((mp, subs, feats), f32),
         "last_send": ((subs, feats), f32),
         "last_land": ((subs, feats), f32),
-        "dn": ((dp, slab, feats // dp), bf16),
-        "dn_land": ((dp, slab, feats // dp), bf16),
+        "dn": ((PLANE, levels, slab - 8, feats // dp), f32),
+        "dn_plane": ((PLANE, levels, slab - 8, feats // dp), f32),
+        "dn_line": ((levels, slab - 8, feats // dp), f32),
+        "dn_land": ((levels, slab - 8, feats // dp), f32),
     }
-    sems = {"ssem": (11,), "rsem": (11,), "msend": (5,), "mrecv": (5,), "csem": (7,)}
+    sems = {"ssem": (14,), "rsem": (14,), "msend": (5,), "mrecv": (5,), "csem": (7,)}
     names = (*inputs, *middle, *scratch, *sems)
     parts = pl.pallas_call(
         functools.partial(step_kernel, dp, mp, subs, rank, names),
@@ -759,7 +794,7 @@
         out_shape=tuple(jax.ShapeDtypeStruct(s, t) for s, t in outputs),
         in_specs=[smem] + [vmem] * len(middle),
         out_specs=(vmem,) * len(outputs),
-        compiler_params=pltpu.CompilerParams(vmem_limit_bytes=32 * 1024 * 1024),
+        compiler_params=pltpu.CompilerParams(vmem_limit_bytes=60 * 1024 * 1024),
     )(lengths[:, 0], *parts)
     loss, query_grad, item_grad, input_grad, key_down, value_down_grad, key_up, value_up = out
     return (

time: 61.5 us -> 57.3 us (0.932)
  local copies, waits for them, and re-layouts: 4.68 us -> 0 us
  Pallas kernels: 55.7 us -> 56.4 us
    unnamed x12 -> x0, local copies, waits for them, and re-layouts: 4.68 us -> none
    pallas_call x1, Pallas kernels: 2.82 us -> 3.66 us  [fused_local(): pl.pallas_call(functools.partial(result_kernel, rank), out_shape=tuple((j...]
where the time goes in v4:
time: 57.3 us; the launch traced here: 57 us
  Pallas kernels  56.4 us (98%)
  between operations  0.65 us (1%)
    pallas_call x1, Pallas kernels, fused_local(): pl.pallas_call(functools.partial(step_kernel, dp, mp, subs, rank, names),...  52.7 us
    pallas_call x1, Pallas kernels, fused_local(): pl.pallas_call(functools.partial(result_kernel, rank), out_shape=tuple((j...  3.66 us

profile of v4, /device:TPU:0, one launch (start us, length us, event | category | flops | bytes accessed | tf_op | source)
XLA Modules:
  0.0 57.0 jit_solution(10758478940535429970)
XLA Ops:
  0.6 52.7 %shard_map.197 = (f32[1,1]{1,0:T(1,128)}, bf16[8,16,256]{2,1,0:T(8,128)(2,1)}, bf16[304,2048]{1,0:T(8,128)(2,1)}, f32[2,2048]{1,0:T(2,128)}, bf16[2,16,48,128]{3...) custom-call(s32[2]{0:T(128)} %bitcast.15, s32[8]{0:T(128)} %refs_1_.1, s32[4,8]{1,0:T(4,128)} %bitcast.14, ...), custom_call_target="tpu_custom_call" | custom-call | tf_op jit(solution)/shard_map/pallas_call | solution.py:781
  53.4 3.7 %shard_map.198 = (f32[1,1]{1,0:T(1,128)}, bf16[8,2048]{1,0:T(8,128)(2,1)}, bf16[8,2048]{1,0:T(8,128)(2,1)}, bf16[304,2048]{1,0:T(8,128)(2,1)}, f32[16,4096]{1,0:...) custom-call(s32[2]{0:T(128)} %bitcast.16, f32[1,1]{1,0:T(1,128)} %get-tuple-element.22.loss_sum, ...), custom_call_target="tpu_custom_call" | custom-call | tf_op jit(solution)/shard_map/pallas_call | solution.py:792

commit v5 on v4

--- a/solution.py
+++ b/solution.py
@@ -564,6 +564,8 @@
     part_copy = mp_copy(M_PART, pbuf, p_land)
     part_copy.start()
 
+    line_start(DZ, DN, dn_plane, dn_line, dn_land)
+
     dp_wait(*qd_args)
     changes = qd_all[...].reshape(dp * subs * blocks, dq)
     block_ids = lax.rem(lax.broadcasted_iota(jnp.int32, (dp * subs * blocks, dq), 0), blocks)
@@ -579,20 +581,19 @@
     lp_args = (LP, lambda t: lp.at[t], lp_land)
     dp_start(*lp_args)
     lp_land[me] = lp[me]
-    line_start(DZ, DN, dn_plane, dn_line, dn_land)
-
-    part_copy.wait()
-
-    def to_sum(cols, share):
-        r["input_sum"][:, cols] = (share.astype(f32) + p_land[:, cols].astype(f32)).astype(bf16)
-
-    portion(core, 0, to_sum)
 
     dn_sum = line_total(DZ, dn_land)
     dn_all[core, me] = jnp.concatenate([dn_sum, jnp.zeros((8, cols), f32)], 0).astype(bf16)
     dng_args = (DNG, lambda t: dn_all.at[core, me], dn_all.at[core])
     dp_start(*dng_args)
 
+
+    part_copy.wait()
+
+    def to_sum(cols, share):
+        r["input_sum"][:, cols] = (share.astype(f32) + p_land[:, cols].astype(f32)).astype(bf16)
+
+    portion(core, 0, to_sum)
 
     by_home(arrived, GB, g_land, per_core)
 

time: 57.3 us -> 57.4 us (level)
  no operation moved by 1% of the time
where the time goes in v5:
time: 57.4 us; the launch traced here: 57.2 us
  Pallas kernels  56.5 us (98%)
  between operations  0.65 us (1%)
    pallas_call x1, Pallas kernels, fused_local(): pl.pallas_call(functools.partial(step_kernel, dp, mp, subs, rank, names),...  52.9 us
    pallas_call x1, Pallas kernels, fused_local(): pl.pallas_call(functools.partial(result_kernel, rank), out_shape=tuple((j...  3.66 us

profile of v5, /device:TPU:0, one launch (start us, length us, event | category | flops | bytes accessed | tf_op | source)
XLA Modules:
  0.0 57.2 jit_solution(11749164404620955771)
XLA Ops:
  0.6 52.9 %shard_map.197 = (f32[1,1]{1,0:T(1,128)}, bf16[8,16,256]{2,1,0:T(8,128)(2,1)}, bf16[304,2048]{1,0:T(8,128)(2,1)}, f32[2,2048]{1,0:T(2,128)}, bf16[2,16,48,128]{3...) custom-call(s32[2]{0:T(128)} %bitcast.15, s32[8]{0:T(128)} %refs_1_.1, s32[4,8]{1,0:T(4,128)} %bitcast.14, ...), custom_call_target="tpu_custom_call" | custom-call | tf_op jit(solution)/shard_map/pallas_call | solution.py:782
  53.5 3.7 %shard_map.198 = (f32[1,1]{1,0:T(1,128)}, bf16[8,2048]{1,0:T(8,128)(2,1)}, bf16[8,2048]{1,0:T(8,128)(2,1)}, bf16[304,2048]{1,0:T(8,128)(2,1)}, f32[16,4096]{1,0:...) custom-call(s32[2]{0:T(128)} %bitcast.16, f32[1,1]{1,0:T(1,128)} %get-tuple-element.22.loss_sum, ...), custom_call_target="tpu_custom_call" | custom-call | tf_op jit(solution)/shard_map/pallas_call | solution.py:793
